TPU v7x, 32 devices: a whole 2x2x4 slice. The times are simulated.
32 devices in a mesh: shard: 4 (over z), replica: 8 (over y, x, core).
Axes of the slice: x: 2, y: 2, z: 4, core: 2. Of those that a mesh axis runs over, the one named last changes fastest.
Arguments:
- tokens: bfloat16 [8, 3072, 1024], P('replica', 'shard'), may hold values from -6 to 6
- seq_lengths: int32 [8, 6], P('replica'), may hold values from 1 to 1536, as said below
- gain_one: bfloat16 [1024], P('shard'), may hold values from 0.5 to 1.5
- in_weight: bfloat16 [3072, 1024], P('shard'), may hold values from -0.1875 to 0.1875
- conv_weight: bfloat16 [1024, 3], P('shard'), may hold values from -3.5 to 3.5
- out_weight: bfloat16 [1024, 1024], P('shard'), may hold values from -0.1875 to 0.1875
- gain_two: bfloat16 [1024], P('shard'), may hold values from 0.5 to 1.5
- gate_weight: bfloat16 [4608, 1024], P('shard'), may hold values from -0.1875 to 0.1875
- up_weight: bfloat16 [4608, 1024], P('shard'), may hold values from -0.1875 to 0.1875
- down_weight: bfloat16 [1024, 4608], P('shard'), may hold values from -0.09375 to 0.09375
- cotangent: bfloat16 [8, 3072, 1024], P('replica', 'shard'), may hold values from -6 to 6
Outputs:
- block_out: bfloat16 [8, 3072, 1024], P('replica', 'shard')
- input_grad: float32 [8, 3072, 1024], P('replica', 'shard')
- gain_one_grad: float32 [1024], P('shard')
- in_weight_grad: float32 [3072, 1024], P('shard')
- conv_weight_grad: float32 [1024, 3], P('shard')
- out_weight_grad: float32 [1024, 1024], P('shard')
- gain_two_grad: float32 [1024], P('shard')
- gate_weight_grad: float32 [4608, 1024], P('shard')
- up_weight_grad: float32 [4608, 1024], P('shard')
- down_weight_grad: float32 [1024, 4608], P('shard')
Inputs may be any that keep to these rules, and one draw needn't show every extreme that they name: `seq_lengths`: in each row the 6 lengths sum to 3072, and the largest is exactly 1536.
All inputs are finite; a program needn't handle non-finite values.
Results may differ from a plain program's by a relative error of at most 0.017.
Values may be sent and summed in bfloat16 or wider, within the bound.
A program may use at most 256 MiB of HBM per device.

v0:
```python
import jax
import jax.numpy as jnp
from jax import lax
from jax.sharding import PartitionSpec as P

NORM_EPS = 1e-05


def shifted(value, axis, steps):
    count = lax.axis_size(axis)
    initial, last = (max(0, -steps), min(count, count - steps))
    return lax.ppermute(value, axis, [(source, source + steps) for source in range(initial, last)])


def times_rows(left_side, weight):
    return lax.dot_general(
        left_side, weight, (((1,), (1,)), ((), ())), preferred_element_type=jnp.float32
    )


def over_rows(left_side, right_side):
    return lax.dot_general(
        left_side, right_side, (((0,), (0,)), ((), ())), preferred_element_type=jnp.float32
    )


def plain_dot(left_side, weight):
    return jnp.dot(left_side, weight, preferred_element_type=jnp.float32)


def starts_of(seq_lens):
    seq_order = lax.iota(jnp.int32, seq_lens.shape[0])
    return jnp.sum(jnp.where(seq_order[None, :] < seq_order[:, None], seq_lens[None, :], 0), axis=1)


def opens_at(positions, starts):
    return jnp.any(positions[:, None] == starts[None, :], axis=1)


def norm_back(grad_rows, values, scale_val, gain_val):
    weighted = grad_rows * gain_val
    inner_mean = jnp.mean(weighted * values, axis=1, keepdims=True)
    cubed = scale_val * scale_val * scale_val
    return (
        scale_val * weighted - values * cubed * inner_mean,
        jnp.sum(grad_rows * values * scale_val, axis=0),
    )


def on_device(
    tokens,
    seq_lengths,
    gain_one,
    in_weight,
    conv_weight,
    out_weight,
    gain_two,
    gate_weight,
    up_weight,
    down_weight,
    cotangent,
):
    gathered = (
        lax.all_gather(gain_one, "shard", axis=0, tiled=True),
        lax.all_gather(in_weight, "shard", axis=0, tiled=True),
        lax.all_gather(conv_weight, "shard", axis=0, tiled=True),
        lax.all_gather(out_weight, "shard", axis=0, tiled=True),
        lax.all_gather(gain_two, "shard", axis=0, tiled=True),
        lax.all_gather(gate_weight, "shard", axis=0, tiled=True),
        lax.all_gather(up_weight, "shard", axis=0, tiled=True),
        lax.all_gather(down_weight, "shard", axis=0, tiled=True),
    )
    gain_first, in_full, taps_full, outw_full, gain_second, gate_full, up_full, down_full = gathered
    model_width = outw_full.shape[0]
    tok_count = tokens.shape[1]
    hidden = tokens[0].astype(jnp.float32)
    starts = starts_of(seq_lengths[0])
    positions = lax.axis_index("shard") * tok_count - 2 + lax.iota(jnp.int32, tok_count + 4)
    opens_here = opens_at(positions, starts)
    opens_prior = opens_at(positions - 1, starts)
    keep_one = jnp.where(opens_here, 0.0, 1.0).astype(jnp.float32)[:, None]
    keep_two = jnp.where(opens_here | opens_prior, 0.0, 1.0).astype(jnp.float32)[:, None]
    gain_a = gain_first.astype(jnp.float32)
    gain_b = gain_second.astype(jnp.float32)
    conv_taps = taps_full.astype(jnp.float32)
    scale_one = lax.rsqrt(jnp.mean(hidden * hidden, axis=1, keepdims=True) + NORM_EPS)
    normed = (hidden * scale_one * gain_a).astype(jnp.bfloat16)
    projected = times_rows(normed, in_full)
    b_part = projected[:, :model_width]
    c_part = projected[:, model_width : 2 * model_width]
    x_part = projected[:, 2 * model_width :]
    gated = (b_part * x_part).astype(jnp.bfloat16)
    rim_rows = shifted(gated[tok_count - 2 :], "shard", 1)
    extended = jnp.concatenate([rim_rows, gated], axis=0).astype(jnp.float32)
    current = extended[2:]
    lag_one = extended[1 : tok_count + 1] * keep_one[2 : tok_count + 2]
    lag_two = extended[:tok_count] * keep_two[2 : tok_count + 2]
    conv_out = conv_taps[:, 2] * current + conv_taps[:, 1] * lag_one + conv_taps[:, 0] * lag_two
    mixed_in = (c_part * conv_out).astype(jnp.bfloat16)
    middle = hidden + times_rows(mixed_in, outw_full)
    scale_two = lax.rsqrt(jnp.mean(middle * middle, axis=1, keepdims=True) + NORM_EPS)
    normed_two = (middle * scale_two * gain_b).astype(jnp.bfloat16)
    gate_val = times_rows(normed_two, gate_full)
    up_val = times_rows(normed_two, up_full)
    sig_val = jax.nn.sigmoid(gate_val)
    silu_val = gate_val * sig_val
    act_val = (silu_val * up_val).astype(jnp.bfloat16)
    result = middle + times_rows(act_val, down_full)
    cot_rows = cotangent[0]
    down_wgrad = over_rows(cot_rows, act_val)
    act_back = plain_dot(cot_rows, down_full)
    gate_back = (act_back * up_val * sig_val * (1.0 + gate_val * (1.0 - sig_val))).astype(
        jnp.bfloat16
    )
    up_back = (act_back * silu_val).astype(jnp.bfloat16)
    gate_wgrad = over_rows(gate_back, normed_two)
    up_wgrad = over_rows(up_back, normed_two)
    normed_two_back = plain_dot(gate_back, gate_full) + plain_dot(up_back, up_full)
    middle_back, gain_two_wgrad = norm_back(normed_two_back, middle, scale_two, gain_b)
    middle_back = middle_back + cot_rows.astype(jnp.float32)
    branch_back = middle_back.astype(jnp.bfloat16)
    outw_wgrad = over_rows(branch_back, mixed_in)
    mixin_back = plain_dot(branch_back, outw_full)
    cpart_back = mixin_back * conv_out
    conv_back = (mixin_back * c_part).astype(jnp.bfloat16)
    after_rows = shifted(conv_back[:2], "shard", -1)
    ahead_rows = jnp.concatenate([conv_back, after_rows], axis=0).astype(jnp.float32)
    conv_here = ahead_rows[:tok_count]
    taps_wgrad = jnp.stack(
        [
            jnp.sum(conv_here * lag_two, axis=0),
            jnp.sum(conv_here * lag_one, axis=0),
            jnp.sum(conv_here * current, axis=0),
        ],
        axis=1,
    )
    gated_back = (
        conv_taps[:, 2] * conv_here
        + conv_taps[:, 1] * ahead_rows[1 : tok_count + 1] * keep_one[3 : tok_count + 3]
        + conv_taps[:, 0] * ahead_rows[2:] * keep_two[4:]
    )
    proj_back = jnp.concatenate(
        [gated_back * x_part, cpart_back, gated_back * b_part], axis=1
    ).astype(jnp.bfloat16)
    in_wgrad = over_rows(proj_back, normed)
    normed_back = plain_dot(proj_back, in_full)
    hidden_back, gain_one_wgrad = norm_back(normed_back, hidden, scale_one, gain_a)
    hidden_back = hidden_back + middle_back
    pieces = (
        lax.psum_scatter(
            gain_one_wgrad.astype(jnp.bfloat16), "shard", scatter_dimension=0, tiled=True
        ).astype(jnp.float32),
        lax.psum_scatter(
            in_wgrad.astype(jnp.bfloat16), "shard", scatter_dimension=0, tiled=True
        ).astype(jnp.float32),
        lax.psum_scatter(
            taps_wgrad.astype(jnp.bfloat16), "shard", scatter_dimension=0, tiled=True
        ).astype(jnp.float32),
        lax.psum_scatter(
            outw_wgrad.astype(jnp.bfloat16), "shard", scatter_dimension=0, tiled=True
        ).astype(jnp.float32),
        lax.psum_scatter(
            gain_two_wgrad.astype(jnp.bfloat16), "shard", scatter_dimension=0, tiled=True
        ).astype(jnp.float32),
        lax.psum_scatter(
            gate_wgrad.astype(jnp.bfloat16), "shard", scatter_dimension=0, tiled=True
        ).astype(jnp.float32),
        lax.psum_scatter(
            up_wgrad.astype(jnp.bfloat16), "shard", scatter_dimension=0, tiled=True
        ).astype(jnp.float32),
        lax.psum_scatter(
            down_wgrad.astype(jnp.bfloat16), "shard", scatter_dimension=0, tiled=True
        ).astype(jnp.float32),
    )
    piece_a, piece_b, piece_c, piece_d, piece_e, piece_f, piece_g, piece_h = pieces
    owned_parts = (
        lax.psum(piece_a.astype(jnp.bfloat16), "replica").astype(jnp.float32),
        lax.psum(piece_b.astype(jnp.bfloat16), "replica").astype(jnp.float32),
        lax.psum(piece_c.astype(jnp.bfloat16), "replica").astype(jnp.float32),
        lax.psum(piece_d.astype(jnp.bfloat16), "replica").astype(jnp.float32),
        lax.psum(piece_e.astype(jnp.bfloat16), "replica").astype(jnp.float32),
        lax.psum(piece_f.astype(jnp.bfloat16), "replica").astype(jnp.float32),
        lax.psum(piece_g.astype(jnp.bfloat16), "replica").astype(jnp.float32),
        lax.psum(piece_h.astype(jnp.bfloat16), "replica").astype(jnp.float32),
    )
    return (
        result.astype(jnp.bfloat16)[None],
        hidden_back[None],
        owned_parts[0],
        owned_parts[1],
        owned_parts[2],
        owned_parts[3],
        owned_parts[4],
        owned_parts[5],
        owned_parts[6],
        owned_parts[7],
    )


def solution(mesh):
    return jax.shard_map(
        on_device,
        mesh=mesh,
        in_specs=(
            P("replica", "shard", None),
            P("replica", None),
            P("shard"),
            P("shard", None),
            P("shard", None),
            P("shard", None),
            P("shard"),
            P("shard", None),
            P("shard", None),
            P("shard", None),
            P("replica", "shard", None),
        ),
        out_specs=(
            P("replica", "shard", None),
            P("replica", "shard", None),
            P("shard"),
            P("shard", None),
            P("shard", None),
            P("shard", None),
            P("shard"),
            P("shard", None),
            P("shard", None),
            P("shard", None),
        ),
        check_vma=False,
    )
```

profile of v0, /device:TPU:1, one launch (start us, length us, event | category | flops | bytes accessed | tf_op | source)
XLA Modules:
  0.0 1562.3 jit_solution(14319366932338688828)
XLA Ops:
  10.7 10.0 all-gather
  20.7 12.4 all_gather.26
  35.0 92.4 %all-gather.8.cloned.1.call-done = bf16[3072,1024]{1,0:T(8,128)(2,1)} async-done(((bf16[768,1024]{1,0:T(8,128)(2,1)}), bf16[3072,1024]{1,0:T(8,128)(2,1)}) %all-gather.8.cloned.1.call-update) | async-done | bytes 6291472 | tf_op jit(solution)/shard_map/all_gather | solution.py:65
  127.4 7.3 fusion.25
  135.3 1.3 collective-permute-start
  136.7 7.0 all-gather.1
  144.2 3.4 multiply_convert_fusion.8
  147.6 25.4 %all-gather.10.cloned.1.call-done = bf16[1024,1024]{1,0:T(8,128)(2,1)} async-done(((bf16[256,1024]{1,0:T(8,128)(2,1)}), bf16[1024,1024]{1,0:T(8,128)(2,1)}) %all-gather.10.cloned.1.call-update) | async-done | bytes 2097168 | tf_op jit(solution)/shard_map/all_gather | solution.py:67
  173.0 4.4 multiply_reduce_fusion.5
  177.5 1.6 copy-done.1
  179.1 1.5 multiply_convert_fusion.7
  180.6 159.8 %all-gather.12.cloned.1.call-done = bf16[4608,1024]{1,0:T(8,128)(2,1)} async-done(((bf16[1152,1024]{1,0:T(8,128)(2,1)}), bf16[4608,1024]{1,0:T(8,128)(2,1)}) %all-gather.12.cloned.1.call-update) | async-done | bytes 9437200 | tf_op jit(solution)/shard_map/all_gather | solution.py:69
  340.4 13.6 fusion.33
  354.0 152.9 %all-gather.14.cloned.1.call-done = bf16[4608,1024]{1,0:T(8,128)(2,1)} async-done(((bf16[1152,1024]{1,0:T(8,128)(2,1)}), bf16[4608,1024]{1,0:T(8,128)(2,1)}) %all-gather.14.cloned.1.call-update) | async-done | bytes 9437200 | tf_op jit(solution)/shard_map/all_gather | solution.py:70
  506.8 13.6 fusion.34
  520.5 152.8 %all-gather.16.cloned.1.call-done = bf16[1024,4608]{1,0:T(8,128)(2,1)} async-done(((bf16[256,4608]{1,0:T(8,128)(2,1)}), bf16[1024,4608]{1,0:T(8,128)(2,1)}) %all-gather.16.cloned.1.call-update) | async-done | bytes 9437200 | tf_op jit(solution)/shard_map/all_gather | solution.py:71
  673.2 27.8 %multiply_convert_fusion = (bf16[768,4608]{1,0:T(8,128)(2,1)}, bf16[768,4608]{1,0:T(8,128)(2,1)}, bf16[768,4608]{1,0:T(8,128)(2,1)}) fusion(f32[768,4608]{1,0:T(8,128)} %fusion.33, f32[768,4608]{1,0:T(8,128)} %fusion.34, bf16[1024,4608]{1,0:T(8,128)(2,1)} %all-gather.16.cloned.1.call-done, bf16[1,768,1024]{2,1,0:T(8,128)(2,1)} %param.21), kind=kOutput, calls=%fused_computation | convolution fusion | flops 7300841472 | bytes 60555264 | tf_op jit(solution)/shard_map/dot_general | solution.py:28
  701.1 12.2 fusion.35
  713.4 10.9 multiply_reduce_fusion
  725.1 1.7 copy-done.4
  726.8 3.2 convolution_convert_fusion.4
  730.0 4.5 fusion.22
  734.6 3.4 multiply_convert_fusion.4
  738.0 1.6 collective-permute-start.1
  739.5 3.5 collective-permute-done.1
  743.5 3.7 multiply_reduce_fusion.3
  749.6 8.9 convolution_convert_fusion.3
  758.5 1.3 copy-done.14
  759.9 13.1 convolution_convert_fusion.2
  773.1 13.2 convolution_convert_fusion.1
  786.4 1.3 copy-done.16
  787.7 13.0 fusion.1
  801.9 82.7 %reduce-scatter.9.cloned.1.call-done = bf16[768,1024]{1,0:T(8,128)(2,1)} async-done(((bf16[3072,1024]{1,0:T(8,128)(2,1)}), bf16[768,1024]{1,0:T(8,128)(2,1)}) %reduce-scatter.9.cloned.1.call-update) | async-done | bytes 1572880 | tf_op jit(solution)/shard_map/reduce_scatter | solution.py:153
  884.6 163.9 %reduce-scatter.13.cloned.1.call-done = bf16[1152,1024]{1,0:T(8,128)(2,1)} async-done(((bf16[4608,1024]{1,0:T(8,128)(2,1)}), bf16[1152,1024]{1,0:T(8,128)(2,1)}) %reduce-scatter.13.cloned.1.call-update) | async-done | bytes 2359312 | tf_op jit(solution)/shard_map/reduce_scatter | solution.py:165
  1048.4 164.6 %reduce-scatter.15.cloned.1.call-done = bf16[1152,1024]{1,0:T(8,128)(2,1)} async-done(((bf16[4608,1024]{1,0:T(8,128)(2,1)}), bf16[1152,1024]{1,0:T(8,128)(2,1)}) %reduce-scatter.15.cloned.1.call-update) | async-done | bytes 2359312 | tf_op jit(solution)/shard_map/reduce_scatter | solution.py:168
  1213.1 164.5 %reduce-scatter.17.cloned.1.call-done = bf16[256,4608]{0,1:T(8,128)(2,1)} async-done(((bf16[1024,4608]{0,1:T(8,128)(2,1)}), bf16[256,4608]{0,1:T(8,128)(2,1)}) %reduce-scatter.17.cloned.1.call-update) | async-done | bytes 2359312 | tf_op jit(solution)/shard_map/reduce_scatter | solution.py:171
  1379.5 13.4 fusion.20
  1392.9 10.0 fusion.11
  1402.9 9.8 all-reduce.4
  1412.9 4.9 fusion.8
  1417.8 0.9 copy.25
  1418.7 14.4 all-reduce.2
  1434.8 105.6 %all-reduce.7.cloned.1.call-done = (bf16[256,4608]{0,1:T(8,128)(2,1)}, bf16[768,1024]{1,0:T(8,128)(2,1)}, bf16[256,1024]{1,0:T(8,128)(2,1)}, bf16[1152,1024]{1,0:T(8,128)(2,1)}, bf16[1152,1024]{1,0:T(8,128)(2,1)}) async-done(((bf16[256,4608]{0,1:T(8,128)(2,1)}, bf16[768,1024]{1,0:T(8,128)(2,1)}, bf16[256,1024]{1,0:T(8,128)(2,1)}, bf16[1152,1024]{1,0:T(8,128)(2,1)}, bf16[1152,1024]{1,0:T(8,128)(2,1)}), ...) | async-done | bytes 9175056 | tf_op jit(solution)/shard_map/psum | solution.py:184
  1540.4 4.5 convert_element_type.148
  1544.9 2.7 convert_element_type.150
  1547.6 3.0 copy.23
  1550.6 3.5 convert_element_type.141
  1554.1 1.1 convert_element_type.144
  (134 shorter events, 14.4 us)
Async XLA Ops:
  7.2 120.2 %all-gather.8.cloned.1.call-start = ((), (), s32[]{:S(2)}) async-start(), calls=%async_computation.6 | async-start | bytes 7864320 | tf_op jit(solution)/shard_map/all_gather | solution.py:65
  7.9 165.1 %all-gather.10.cloned.1.call-start = ((), (), s32[]{:S(2)}) async-start(), calls=%async_computation.7 | async-start | bytes 2621440 | tf_op jit(solution)/shard_map/all_gather | solution.py:67
  8.7 2.0 copy-start.31
  8.7 12.0 copy-start.29
  8.7 24.4 %copy-start.32 = (s32[1,6]{1,0:T(1,128)S(1)}, s32[1,6]{1,0:T(1,128)}, u32[]{:S(2)}) copy-start(s32[1,6]{1,0:T(1,128)} %param.12) | copy-start | bytes 76
  8.7 24.6 %copy-start.7 = (bf16[1,768,1024]{2,1,0:T(8,128)(2,1)S(1)}, bf16[1,768,1024]{2,1,0:T(8,128)(2,1)}, u32[]{:S(2)}) copy-start(bf16[1,768,1024]{2,1,0:T(8,128)(2,1)} %param.11) | copy-start | bytes 4718596
  8.7 331.7 %all-gather.12.cloned.1.call-start = ((), (), s32[]{:S(2)}) async-start(), calls=%async_computation.8 | async-start | bytes 11796480 | tf_op jit(solution)/shard_map/all_gather | solution.py:69
  9.4 497.4 %all-gather.14.cloned.1.call-start = ((), (), s32[]{:S(2)}) async-start(), calls=%async_computation.9 | async-start | bytes 11796480 | tf_op jit(solution)/shard_map/all_gather | solution.py:70
  10.0 663.2 %all-gather.16.cloned.1.call-start = ((), (), s32[]{:S(2)}) async-start(), calls=%async_computation.10 | async-start | bytes 11796480 | tf_op jit(solution)/shard_map/all_gather | solution.py:71
  10.6 791.3 %reduce-scatter.11.cloned.1.call-start = ((), (), s32[]{:S(2)}) async-start(), calls=%async_computation.12 | async-start | bytes 2621440 | tf_op jit(solution)/shard_map/reduce_scatter | solution.py:159
  20.7 114.1 %copy-start.26 = (f32[4,1,256]{2,1,0:T(1,128)}, f32[4,1,256]{2,1,0:T(1,128)S(1)}, u32[]{:S(2)}) copy-start(f32[4,1,256]{2,1,0:T(1,128)S(1)} %convert_element_type.155) | copy-start | bytes 12292
  34.3 100.4 %copy-start.24 = (f32[768]{0:T(1024)}, f32[768]{0:T(1024)S(1)}, u32[]{:S(2)}) copy-start(f32[768]{0:T(1024)S(1)} %get-tuple-element.74) | copy-start | bytes 9220
  134.8 9.4 copy-start
  134.8 1.9 copy-start.33
  135.3 8.4 collective-permute-start
  177.5 1.7 copy-start.1
  701.1 12.3 copy-start.2
  701.1 12.3 copy-start.30
  713.4 10.9 copy-start.15
  724.3 2.5 copy-start.21
  725.1 1.7 copy-start.4
  730.0 154.6 %reduce-scatter.9.cloned.1.call-start = ((), (), s32[]{:S(2)}) async-start(), calls=%async_computation.11 | async-start | bytes 7864320 | tf_op jit(solution)/shard_map/reduce_scatter | solution.py:153
  730.0 4.5 copy-start.6
  734.5 8.9 slice-start
  734.5 8.9 slice-start.1
  734.5 8.9 slice-start.2
  737.9 10.1 copy-start.12
  738.0 5.5 copy-start.28
  738.0 5.1 collective-permute-start.1
  747.2 2.4 copy-start.8
  747.2 2.4 copy-start.25
  747.2 2.3 copy-start.27
  758.5 1.4 copy-start.14
  758.5 290.0 %reduce-scatter.13.cloned.1.call-start = ((), (), s32[]{:S(2)}) async-start(), calls=%async_computation.13 | async-start | bytes 11796480 | tf_op jit(solution)/shard_map/reduce_scatter | solution.py:165
  773.0 440.1 %reduce-scatter.15.cloned.1.call-start = ((), (), s32[]{:S(2)}) async-start(), calls=%async_computation.14 | async-start | bytes 11796480 | tf_op jit(solution)/shard_map/reduce_scatter | solution.py:168
  786.3 591.2 %reduce-scatter.17.cloned.1.call-start = ((), (), s32[]{:S(2)}) async-start(), calls=%async_computation.15 | async-start | bytes 11796480 | tf_op jit(solution)/shard_map/reduce_scatter | solution.py:171
  800.8 617.0 %reduce-scatter.19.cloned.1.call-start = ((), (), s32[]{:S(2)}) async-start(), calls=%async_computation.16 | async-start | bytes 327680
  801.8 738.6 %all-reduce.7.cloned.1.call-start = ((), (), s32[]{:S(2)}) async-start(), calls=%async_computation.17 | async-start | bytes 18350080 | tf_op jit(solution)/shard_map/psum | solution.py:184
  1377.6 1.9 copy-start.3
  1379.5 13.4 copy-start.9
  1379.5 13.4 copy-start.13
  1379.5 13.4 copy-start.18
  1379.5 13.4 copy-start.20
  1392.9 20.0 %copy-start.5 = (f32[768,1024]{1,0:T(8,128)S(1)}, f32[768,1024]{1,0:T(8,128)}, u32[]{:S(2)}) copy-start(f32[768,1024]{1,0:T(8,128)} %copy-done.4) | copy-start | bytes 9437188
  1392.9 20.0 %copy-start.23 = (f32[768]{0:T(1024)S(1)}, f32[768]{0:T(1024)}, u32[]{:S(2)}) copy-start(f32[768]{0:T(1024)} %get-tuple-element.73) | copy-start | bytes 9220
  1540.4 4.5 copy-start.11
  1544.9 2.7 copy-start.10
  1550.6 3.5 copy-start.22
  (4 other events, 4.6 us)
Sparse Core Ops, SparseCore 0:
  9.6 117.7 all-gather.7
  129.0 43.9 all-gather.9
  174.6 165.7 all-gather.11
  341.8 164.9 all-gather.13
  508.2 164.9 all-gather.15
  730.1 41.7 reduce-scatter.10
  774.3 110.2 reduce-scatter.8
  887.0 161.3 reduce-scatter.12
  1050.9 162.1 reduce-scatter.14
  1215.4 162.1 reduce-scatter.16
  1380.5 19.2 reduce-scatter.18
  1404.1 136.2 all-reduce.6
where the time goes:
time: 1570 us; the launch traced here: 1560 us
  waiting for transfers between devices  1270 us (81%)
  matrix products  169 us (11%)
  blocking collectives  53.6 us (3%)
  other arithmetic  34.7 us (2%)
    reduce_scatter x1, waiting for transfers between devices, on_device(): lax.psum_scatter(up_wgrad.astype(jnp.bfloat16), 'shard', scatter_dimensio...  165 us
    reduce_scatter x1, waiting for transfers between devices, on_device(): lax.psum_scatter(down_wgrad.astype(jnp.bfloat16), 'shard', scatter_dimens...  164 us
    reduce_scatter x1, waiting for transfers between devices, on_device(): lax.psum_scatter(gate_wgrad.astype(jnp.bfloat16), 'shard', scatter_dimens...  164 us
    all_gather x1, waiting for transfers between devices, on_device(): lax.all_gather(gate_weight, 'shard', axis=0, tiled=True)  160 us
    all_gather x1, waiting for transfers between devices, on_device(): lax.all_gather(up_weight, 'shard', axis=0, tiled=True)  153 us
    all_gather x1, waiting for transfers between devices, on_device(): lax.all_gather(down_weight, 'shard', axis=0, tiled=True)  153 us
    psum x1, waiting for transfers between devices, on_device(): lax.psum(piece_h.astype(jnp.bfloat16), 'replica').astype(jnp.float32)  106 us
    all_gather x1, waiting for transfers between devices, on_device(): lax.all_gather(in_weight, 'shard', axis=0, tiled=True)  92.4 us
  transfers between devices with their start and end apart: 14, of which 11 were waited for; matrix products, arithmetic and copies ran while one was open for 9% of the time, Pallas kernels for 0%

commit v1 on v0

--- a/solution.py
+++ b/solution.py
@@ -45,6 +45,110 @@
         scale_val * weighted - values * cubed * inner_mean,
         jnp.sum(grad_rows * values * scale_val, axis=0),
     )
+
+
+def bits_of(count):
+    return [1 << place for place in range(count.bit_length() - 1)]
+
+
+def swap(value, axis, bit):
+    count = lax.axis_size(axis)
+    return lax.ppermute(value, axis, [(source, source ^ bit) for source in range(count)])
+
+
+def route(order):
+    far = [("replica", bit) for bit in bits_of(lax.axis_size("replica"))[1:]]
+    if order:
+        far = far[::-1]
+    return far
+
+
+def shard_route():
+    return [("shard", bit) for bit in bits_of(lax.axis_size("shard"))]
+
+
+CORE = [("replica", 1)]
+
+
+def own_bit(axis, bit):
+    return (lax.axis_index(axis) // bit) % 2
+
+
+def place_dims(rows):
+    shards, replicas = lax.axis_size("shard"), lax.axis_size("replica")
+    depth = len(bits_of(shards)) + len(bits_of(replicas))
+    return (2,) * depth, rows // (shards * replicas)
+
+
+def dim_of(axis, bit, held):
+    full = [("shard", b) for b in bits_of(lax.axis_size("shard"))[::-1]]
+    full = full + [("replica", b) for b in bits_of(lax.axis_size("replica"))[::-1]]
+    return sum(1 for item in full[: full.index((axis, bit))] if item in held)
+
+
+def spread(block, hops, held):
+    held = list(held)
+    for axis, bit in hops:
+        other = swap(block, axis, bit)
+        dim = dim_of(axis, bit, held)
+        shape = block.shape[:dim] + (2,) + block.shape[dim:]
+        mine = lax.broadcasted_iota(jnp.int32, shape, dim) == own_bit(axis, bit)
+        block = jnp.where(mine, jnp.expand_dims(block, dim), jnp.expand_dims(other, dim))
+        held.append((axis, bit))
+    return block
+
+
+def gather_rows(block, order):
+    replicas = lax.axis_size("replica")
+    rows = block.shape[0] // replicas
+    piece = lax.dynamic_slice_in_dim(block, lax.axis_index("replica") * rows, rows, 0)
+    whole = spread(piece, shard_route() + route(order) + CORE, [])
+    return whole.reshape((-1, block.shape[1]))
+
+
+class Reduction:
+    def __init__(self, grad, order):
+        dims, rows = place_dims(grad.shape[0])
+        self.width = grad.shape[1]
+        self.value = grad.astype(jnp.bfloat16).reshape(dims + (rows, self.width))
+        self.held = shard_route() + CORE + route(order)
+        self.down = CORE + route(order) + shard_route()[::-1]
+        self.up = route(1 - order) + CORE
+
+    def live(self):
+        return bool(self.down or self.up)
+
+    def step(self):
+        if self.down:
+            axis, bit = self.down.pop(0)
+            self.held.remove((axis, bit))
+            dim = dim_of(axis, bit, self.held)
+            side = own_bit(axis, bit)
+            away = lax.dynamic_index_in_dim(self.value, 1 - side, dim, keepdims=False)
+            here = lax.dynamic_index_in_dim(self.value, side, dim, keepdims=False)
+            came = swap(away, axis, bit)
+            total = here.astype(jnp.float32) + came.astype(jnp.float32)
+            self.value = total.astype(jnp.bfloat16)
+        elif self.up:
+            hop = self.up.pop(0)
+            self.value = spread(self.value, [hop], self.held)
+            self.held.append(hop)
+
+    def result(self):
+        return self.value.reshape((-1, self.width)).astype(jnp.float32)
+
+
+def tie(values, *reductions):
+    out = lax.optimization_barrier(tuple(values) + tuple(one.value for one in reductions))
+    for one, value in zip(reductions, out[len(values):]):
+        one.value = value
+    return out[: len(values)]
+
+
+def total_of(value):
+    for axis, bit in CORE + route(0) + shard_route():
+        value = value + swap(value, axis, bit)
+    return value
 
 
 def on_device(
@@ -60,17 +164,16 @@
     down_weight,
     cotangent,
 ):
-    gathered = (
-        lax.all_gather(gain_one, "shard", axis=0, tiled=True),
-        lax.all_gather(in_weight, "shard", axis=0, tiled=True),
-        lax.all_gather(conv_weight, "shard", axis=0, tiled=True),
-        lax.all_gather(out_weight, "shard", axis=0, tiled=True),
-        lax.all_gather(gain_two, "shard", axis=0, tiled=True),
-        lax.all_gather(gate_weight, "shard", axis=0, tiled=True),
-        lax.all_gather(up_weight, "shard", axis=0, tiled=True),
-        lax.all_gather(down_weight, "shard", axis=0, tiled=True),
-    )
-    gain_first, in_full, taps_full, outw_full, gain_second, gate_full, up_full, down_full = gathered
+    own_width = gain_one.shape[0]
+    slim = jnp.concatenate([gain_one[None], gain_two[None], conv_weight.T], axis=0)
+    slim = spread(slim, shard_route(), [])
+    slim = slim.reshape((-1,) + slim.shape[-2:]).swapaxes(0, 1).reshape(slim.shape[-2], -1)
+    gain_first, gain_second, taps_full = slim[0], slim[1], slim[2:].T
+    in_full = gather_rows(in_weight, 1)
+    outw_full = gather_rows(out_weight, 0)
+    gate_full = gather_rows(gate_weight, 1)
+    up_full = gather_rows(up_weight, 0)
+    down_full = gather_rows(down_weight, 0)
     model_width = outw_full.shape[0]
     tok_count = tokens.shape[1]
     hidden = tokens[0].astype(jnp.float32)
@@ -105,21 +208,37 @@
     sig_val = jax.nn.sigmoid(gate_val)
     silu_val = gate_val * sig_val
     act_val = (silu_val * up_val).astype(jnp.bfloat16)
-    result = middle + times_rows(act_val, down_full)
     cot_rows = cotangent[0]
     down_wgrad = over_rows(cot_rows, act_val)
-    act_back = plain_dot(cot_rows, down_full)
+    down_red = Reduction(down_wgrad, 0)
+    (cot_back,) = tie((cot_rows,), down_red)
+    act_back = plain_dot(cot_back, down_full)
+    down_red.step()
     gate_back = (act_back * up_val * sig_val * (1.0 + gate_val * (1.0 - sig_val))).astype(
         jnp.bfloat16
     )
     up_back = (act_back * silu_val).astype(jnp.bfloat16)
-    gate_wgrad = over_rows(gate_back, normed_two)
-    up_wgrad = over_rows(up_back, normed_two)
-    normed_two_back = plain_dot(gate_back, gate_full) + plain_dot(up_back, up_full)
+    gate_back, up_back = tie((gate_back, up_back), down_red)
+    down_red.step()
+    gate_red = Reduction(over_rows(gate_back, normed_two), 1)
+    (up_back,) = tie((up_back,), gate_red)
+    gate_red.step()
+    up_red = Reduction(over_rows(up_back, normed_two), 0)
+    up_back, gate_back = tie((up_back, gate_back), gate_red, up_red)
+    gate_red.step()
+    up_red.step()
+    gate_part = plain_dot(gate_back, gate_full)
+    gate_part, up_back = tie((gate_part, up_back), up_red)
+    up_red.step()
+    normed_two_back = gate_part + plain_dot(up_back, up_full)
+    (normed_two_back,) = tie((normed_two_back,), down_red)
+    down_red.step()
     middle_back, gain_two_wgrad = norm_back(normed_two_back, middle, scale_two, gain_b)
     middle_back = middle_back + cot_rows.astype(jnp.float32)
     branch_back = middle_back.astype(jnp.bfloat16)
-    outw_wgrad = over_rows(branch_back, mixed_in)
+    out_red = Reduction(over_rows(branch_back, mixed_in), 1)
+    (branch_back,) = tie((branch_back,), out_red)
+    out_red.step()
     mixin_back = plain_dot(branch_back, outw_full)
     cpart_back = mixin_back * conv_out
     conv_back = (mixin_back * c_part).astype(jnp.bfloat16)
@@ -142,46 +261,38 @@
     proj_back = jnp.concatenate(
         [gated_back * x_part, cpart_back, gated_back * b_part], axis=1
     ).astype(jnp.bfloat16)
-    in_wgrad = over_rows(proj_back, normed)
+    (proj_back,) = tie((proj_back,), out_red, down_red, gate_red)
+    out_red.step()
+    down_red.step()
+    gate_red.step()
+    in_red = Reduction(over_rows(proj_back, normed), 1)
+    proj_back, act_val = tie((proj_back, act_val), in_red)
+    in_red.step()
     normed_back = plain_dot(proj_back, in_full)
     hidden_back, gain_one_wgrad = norm_back(normed_back, hidden, scale_one, gain_a)
     hidden_back = hidden_back + middle_back
-    pieces = (
-        lax.psum_scatter(
-            gain_one_wgrad.astype(jnp.bfloat16), "shard", scatter_dimension=0, tiled=True
-        ).astype(jnp.float32),
-        lax.psum_scatter(
-            in_wgrad.astype(jnp.bfloat16), "shard", scatter_dimension=0, tiled=True
-        ).astype(jnp.float32),
-        lax.psum_scatter(
-            taps_wgrad.astype(jnp.bfloat16), "shard", scatter_dimension=0, tiled=True
-        ).astype(jnp.float32),
-        lax.psum_scatter(
-            outw_wgrad.astype(jnp.bfloat16), "shard", scatter_dimension=0, tiled=True
-        ).astype(jnp.float32),
-        lax.psum_scatter(
-            gain_two_wgrad.astype(jnp.bfloat16), "shard", scatter_dimension=0, tiled=True
-        ).astype(jnp.float32),
-        lax.psum_scatter(
-            gate_wgrad.astype(jnp.bfloat16), "shard", scatter_dimension=0, tiled=True
-        ).astype(jnp.float32),
-        lax.psum_scatter(
-            up_wgrad.astype(jnp.bfloat16), "shard", scatter_dimension=0, tiled=True
-        ).astype(jnp.float32),
-        lax.psum_scatter(
-            down_wgrad.astype(jnp.bfloat16), "shard", scatter_dimension=0, tiled=True
-        ).astype(jnp.float32),
-    )
-    piece_a, piece_b, piece_c, piece_d, piece_e, piece_f, piece_g, piece_h = pieces
+    every = [down_red, gate_red, up_red, out_red, in_red]
+    (normed_back, act_val) = tie((normed_back, act_val), *every)
+    result = middle + times_rows(act_val, down_full)
+    while any(one.live() for one in every):
+        busy = [one for one in every if one.live()]
+        for one in busy:
+            one.step()
+        tie((), *busy)
+    slim_grads = jnp.concatenate([gain_one_wgrad[None], gain_two_wgrad[None], taps_wgrad.T], axis=0)
+    slim_grads = total_of(slim_grads)
+    slim_grads = lax.dynamic_slice_in_dim(
+        slim_grads, lax.axis_index("shard") * own_width, own_width, 1
+    )
     owned_parts = (
-        lax.psum(piece_a.astype(jnp.bfloat16), "replica").astype(jnp.float32),
-        lax.psum(piece_b.astype(jnp.bfloat16), "replica").astype(jnp.float32),
-        lax.psum(piece_c.astype(jnp.bfloat16), "replica").astype(jnp.float32),
-        lax.psum(piece_d.astype(jnp.bfloat16), "replica").astype(jnp.float32),
-        lax.psum(piece_e.astype(jnp.bfloat16), "replica").astype(jnp.float32),
-        lax.psum(piece_f.astype(jnp.bfloat16), "replica").astype(jnp.float32),
-        lax.psum(piece_g.astype(jnp.bfloat16), "replica").astype(jnp.float32),
-        lax.psum(piece_h.astype(jnp.bfloat16), "replica").astype(jnp.float32),
+        slim_grads[0],
+        in_red.result(),
+        slim_grads[2:].T,
+        out_red.result(),
+        slim_grads[1],
+        gate_red.result(),
+        up_red.result(),
+        down_red.result(),
     )
     return (
         result.astype(jnp.bfloat16)[None],

time: 1570 us -> 836 us (0.53)
  waiting for transfers between devices: 1270 us -> 345 us
  starting transfers between devices: 3.32 us -> 169 us
  other arithmetic: 34.7 us -> 125 us
  blocking collectives: 53.6 us -> 0 us
  local copies, waits for them, and re-layouts: 14.5 us -> 41.7 us
  matrix products: 169 us -> 145 us
    all_gather x5 -> x0, waiting for transfers between devices: 583 us -> none  [the longest x1 160 us: on_device(): lax.all_gather(gate_weight, 'shard', axis=0, tiled=True)]
    reduce_scatter x5 -> x0, waiting for transfers between devices: 576 us -> none  [the longest x1 165 us: on_device(): lax.psum_scatter(up_wgrad.astype(jnp.bfloat16), 'shard', scatter_dimensio...]
    ppermute x0 -> x72, waiting for transfers between devices: none -> 340 us  [swap(): lax.ppermute(value, axis, [(source, source ^ bit) for source in range(cou...]
    ppermute x0 -> x72, starting transfers between devices: none -> 143 us  [swap(): lax.ppermute(value, axis, [(source, source ^ bit) for source in range(cou...]
    psum x1 -> x0, waiting for transfers between devices: 106 us -> none  [on_device(): lax.psum(piece_h.astype(jnp.bfloat16), 'replica').astype(jnp.float32)]
    select_n x0 -> x40, other arithmetic: none -> 48 us  [spread(): jnp.where(mine, jnp.expand_dims(block, dim), jnp.expand_dims(other, dim))]
    convert_element_type x8 -> x32, other arithmetic: 13.6 us -> 57.1 us  [the longest x25 43 us: step(): self.value = total.astype(jnp.bfloat16)]
    all_gather x3 -> x0, blocking collectives: 29.4 us -> none  [the longest x1 12.4 us: on_device(): lax.all_gather(conv_weight, 'shard', axis=0, tiled=True)]
  transfers between devices with their start and end apart: 14 -> 74, of which waited for: 11 -> 31; matrix products, arithmetic and copies ran while one was open for 9% -> 30% of each run, Pallas kernels for 0% -> 0%
where the time goes in v1:
time: 836 us; the launch traced here: 828 us
  waiting for transfers between devices  345 us (41%)
  starting transfers between devices  169 us (20%)
  matrix products  145 us (17%)
  other arithmetic  125 us (15%)
  local copies, waits for them, and re-layouts  41.7 us (5%)
    ppermute x72, waiting for transfers between devices, swap(): lax.ppermute(value, axis, [(source, source ^ bit) for source in range(cou...  340 us
    ppermute x72, starting transfers between devices, swap(): lax.ppermute(value, axis, [(source, source ^ bit) for source in range(cou...  143 us
    dot_general x5, matrix products, plain_dot(): return jnp.dot(left_side, weight, preferred_element_type=jnp.float32)  56.8 us
    dot_general x5, matrix products, times_rows(): lax.dot_general(left_side, weight, (((1,), (1,)), ((), ())), preferred_el...  50.6 us
    select_n x40, other arithmetic, spread(): jnp.where(mine, jnp.expand_dims(block, dim), jnp.expand_dims(other, dim))  48 us
    convert_element_type x25, other arithmetic, step(): self.value = total.astype(jnp.bfloat16)  43 us
    dot_general x5, matrix products, over_rows(): lax.dot_general(left_side, right_side, (((0,), (0,)), ((), ())), preferre...  37.9 us
    ppermute x2, starting transfers between devices, shifted(): lax.ppermute(value, axis, [(source, source + steps) for source in range(i...  25.7 us
  transfers between devices with their start and end apart: 74, of which 31 were waited for; matrix products, arithmetic and copies ran while one was open for 30% of the time, Pallas kernels for 0%

profile of v1, /device:TPU:1, one launch (start us, length us, event | category | flops | bytes accessed | tf_op | source)
XLA Modules:
  0.0 828.1 jit_solution(3319949911018928143)
XLA Ops:
  17.4 4.5 collective-permute-done
  36.9 27.7 %collective-permute-done.3 = bf16[2,96,1024]{2,1,0:T(8,128)(2,1)S(1)} collective-permute-done((bf16[2,96,1024]{2,1,0:T(8,128)(2,1)S(1)}, bf16[2,96,1024]{2,1,0:T(8,128)(2,1)S(1)}, u32[]{:S(2)}, u32[]{:S(2)}) %collective-permute-start.3) | collective-permute-done | bytes 393248 | tf_op jit(solution)/shard_map/ppermute | solution.py:56
  66.6 10.5 %collective-permute-done.14 = bf16[2,144,1024]{2,1,0:T(8,128)(2,1)S(1)} collective-permute-done((bf16[2,144,1024]{2,1,0:T(8,128)(2,1)S(1)}, bf16[2,144,1024]{2,1,0:T(8,128)(2,1)S(1)}, u32[]{:S(2)}, u32[]{:S(2)}) %collective-permute-start.14) | collective-permute-done | bytes 589856 | tf_op jit(solution)/shard_map/ppermute | solution.py:56
  77.2 12.6 %collective-permute-done.19 = bf16[2,144,1024]{2,1,0:T(8,128)(2,1)S(1)} collective-permute-done((bf16[2,144,1024]{2,1,0:T(8,128)(2,1)S(1)}, bf16[2,144,1024]{2,1,0:T(8,128)(2,1)S(1)}, u32[]{:S(2)}, u32[]{:S(2)}) %collective-permute-start.19) | collective-permute-done | bytes 589856 | tf_op jit(solution)/shard_map/ppermute | solution.py:56
  93.2 34.5 %collective-permute-done.24 = bf16[2,32,4608]{2,1,0:T(8,128)(2,1)S(1)} collective-permute-done((bf16[2,32,4608]{2,1,0:T(8,128)(2,1)S(1)}, bf16[2,32,4608]{2,1,0:T(8,128)(2,1)S(1)}, u32[]{:S(2)}, u32[]{:S(2)}) %collective-permute-start.24) | collective-permute-done | bytes 589856 | tf_op jit(solution)/shard_map/ppermute | solution.py:56
  133.0 45.2 %collective-permute-start.6 = (bf16[2,2,2,2,96,1024]{5,4,3,2,1,0:T(8,128)(2,1)S(1)}, bf16[2,2,2,2,96,1024]{5,4,3,2,1,0:T(8,128)(2,1)S(1)}, u32[]{:S(2)}, u32[]{:S(2)}) collective-permute-start(bf16[2,2,2,2,96,1024]{5,4,3,2,1,0:T(8,128)(2,1)S(1)} %broadcast_select_fusion.4), channel_id=1, source_target_pairs={{0,1},{1,0},{2,3},{3,2},{4,5},{5,4},{6,7},{7,6},{8,9},{9,8},{10,11... | collective-permute-start | bytes 9437192 | tf_op jit(solution)/shard_map/ppermute | solution.py:56
  183.3 23.4 %collective-permute-done.16 = bf16[2,2,2,144,1024]{4,3,2,1,0:T(8,128)(2,1)S(1)} collective-permute-done((bf16[2,2,2,144,1024]{4,3,2,1,0:T(8,128)(2,1)S(1)}, bf16[2,2,2,144,1024]{4,3,2,1,0:T(8,128)(2,1)S(1)}, u32[]{:S(2)}, u32[]{:S(2)}) %collective-permute-start.16) | collective-permute-done | bytes 2359328 | tf_op jit(solution)/shard_map/ppermute | solution.py:56
  209.3 23.6 %collective-permute-start.17 = (bf16[2,2,2,2,144,1024]{5,4,3,2,1,0:T(8,128)(2,1)}, bf16[2,2,2,2,144,1024]{5,4,3,2,1,0:T(8,128)(2,1)}, u32[]{:S(2)}, u32[]{:S(2)}) collective-permute-start(bf16[2,2,2,2,144,1024]{5,4,3,2,1,0:T(8,128)(2,1)} %broadcast_select_fusion.3), channel_id=1, source_target_pairs={{0,1},{1,0},{2,3},{3,2},{4,5},{5,4},{6,7},{7,6},{8,9},{9,8},{10,11... | collective-permute-start | bytes 14155784 | tf_op jit(solution)/shard_map/ppermute | solution.py:56
  232.9 4.4 broadcast_select_fusion.2
  240.7 7.8 fusion.36
  249.1 24.4 %collective-permute-start.7 = (bf16[2,1024]{1,0:T(2,128)(2,1)S(1)}, bf16[2,1024]{1,0:T(2,128)(2,1)S(1)}, u32[]{:S(2)}, u32[]{:S(2)}) collective-permute-start(bf16[2,1024]{1,0:T(2,128)(2,1)S(1)} %slice.112), channel_id=1, source_target_pairs={{0,8},{8,16},{16,24},{1,9},{9,17},{17,25},{2,10},{10,18},{18,26},{... | collective-permute-start | bytes 12296 | tf_op jit(solution)/shard_map/ppermute | solution.py:12
  273.5 8.5 %collective-permute-done.26 = bf16[2,2,2,32,4608]{4,3,2,1,0:T(8,128)(2,1)} collective-permute-done((bf16[2,2,2,32,4608]{4,3,2,1,0:T(8,128)(2,1)}, bf16[2,2,2,32,4608]{4,3,2,1,0:T(8,128)(2,1)}, u32[]{:S(2)}, u32[]{:S(2)}) %collective-permute-start.26) | collective-permute-done | bytes 2359328 | tf_op jit(solution)/shard_map/ppermute | solution.py:56
  282.0 5.0 broadcast_select_fusion.1
  297.1 11.4 %bitcast_select_fusion.1 = (bf16[4608,1024]{1,0:T(8,128)(2,1)}, bf16[4608,1024]{1,0:T(8,128)(2,1)S(1)}) fusion(pred[4608]{0:T(1024)(128)(4,1)S(1)} %iota.225, bf16[2,2,2,2,144,1024]{5,4,3,2,1,0:T(8,128)(2,1)} %collective-permute-done.22, bf16[2,2,2,2,144,1024]{5,4,3,2,1,0:T(8,128)(2,1)} %broadcast_select_fusion.2, ...), kind=kLoop, calls=%fused_computation.15 | loop fusion | flops 9437184 | bytes 37753344 | tf_op jit(solution)/shard_map/jit(_where)/select_n | solution.py:96
  308.5 10.2 %fusion.66 = f32[768,4608]{1,0:T(8,128)} fusion(bf16[768,1024]{1,0:T(8,128)(2,1)S(1)} %multiply_convert_fusion.7, bf16[4608,1024]{1,0:T(8,128)(2,1)S(1)} %get-tuple-element.155), kind=kOutput, calls=%fused_computation.228 | convolution fusion | flops 7247757312 | bytes 25165824 | tf_op jit(solution)/shard_map/dot_general | solution.py:16
  318.7 20.1 %multiply_convert_fusion.2 = (bf16[768,4608]{1,0:T(8,128)(2,1)}, f32[768,4608]{1,0:T(8,128)}) fusion(f32[768,4608]{1,0:T(8,128)} %fusion.66, bf16[768,1024]{1,0:T(8,128)(2,1)S(1)} %multiply_convert_fusion.7, bf16[4608,1024]{1,0:T(8,128)(2,1)} %get-tuple-element.154), kind=kOutput, calls=%fused_computation.2 | convolution fusion | flops 7268990976 | bytes 46399488 | tf_op jit(solution)/shard_map/dot_general | solution.py:16
  338.8 11.0 %convolution_convert_fusion.2 = bf16[4608,1024]{0,1:T(8,128)(2,1)S(1)} fusion(bf16[768,4608]{1,0:T(8,128)(2,1)} %get-tuple-element.93, bf16[1,768,1024]{2,1,0:T(8,128)(2,1)S(1)} %copy-done.26), kind=kOutput, calls=%fused_computation.7 | convolution fusion | flops 7252475904 | bytes 18087936 | tf_op jit(solution)/shard_map/dot_general | solution.py:22
  354.8 7.8 bitcast_select_fusion
  362.6 22.6 %multiply_convert_fusion = (bf16[768,4608]{1,0:T(8,128)(2,1)}, bf16[768,4608]{1,0:T(8,128)(2,1)}) fusion(f32[768,4608]{1,0:T(8,128)} %fusion.66, f32[768,4608]{1,0:T(8,128)} %get-tuple-element.173, bf16[768,1024]{1,0:T(8,128)(2,1)S(1)} %bitcast.290, bf16[1024,4608]{1,0:T(8,128)(2,1)} %bitcast_select_fusion), kind=kOutput, calls=%fused_computation | convolution fusion | flops 7293763584 | bytes 53477376 | tf_op jit(solution)/shard_map/dot_general | solution.py:28
  385.2 7.5 fusion.3
  392.7 8.4 %convolution_convert_fusion.1 = bf16[4608,1024]{1,0:T(8,128)(2,1)S(1)} fusion(bf16[768,4608]{1,0:T(8,128)(2,1)S(1)} %copy-done.60, bf16[768,1024]{1,0:T(8,128)(2,1)S(1)} %multiply_convert_fusion.7), kind=kOutput, calls=%fused_computation.6 | convolution fusion | flops 7252475904 | bytes 18087936 | tf_op jit(solution)/shard_map/dot_general | solution.py:22
  411.2 10.6 %convolution_convert_fusion = bf16[4608,1024]{1,0:T(8,128)(2,1)S(1)} fusion(bf16[768,4608]{1,0:T(8,128)(2,1)} %get-tuple-element.78, bf16[768,1024]{1,0:T(8,128)(2,1)} %copy-done.28), kind=kOutput, calls=%fused_computation.5 | convolution fusion | flops 7252475904 | bytes 18087936 | tf_op jit(solution)/shard_map/dot_general | solution.py:22
  421.8 10.3 %fusion.2 = bf16[2,2,2,2,144,1024]{5,4,3,2,1,0:T(8,128)(2,1)} fusion(bf16[2,2,2,2,144,1024]{5,4,3,2,1,0:T(8,128)(2,1)} %collective-permute-done.29, bf16[2,2,2,2,2,144,1024]{6,5,4,3,2,1,0:T(8,128)(2,1)S(1)} %bitcast.282, s32[]{:T(128)S(6)} %select_n.631), kind=kLoop, calls=%fused_computation.11 | loop fusion | flops 9437184 | bytes 14155780 | tf_op jit(solution)/shard_map/convert_element_type | solution.py:131
  435.1 5.1 bitcast_select_fusion.3
  442.2 20.9 %collective-permute-done.31 = bf16[2,2,2,32,4608]{4,3,2,1,0:T(8,128)(2,1)} collective-permute-done((bf16[2,2,2,32,4608]{4,3,2,1,0:T(8,128)(2,1)}, bf16[2,2,2,32,4608]{4,3,2,1,0:T(8,128)(2,1)}, u32[]{:S(2)}, u32[]{:S(2)}) %collective-permute-start.31) | collective-permute-done | bytes 2359328 | tf_op jit(solution)/shard_map/ppermute | solution.py:56
  466.3 13.1 %fusion.67 = f32[768,1024]{1,0:T(8,128)S(1)} fusion(bf16[768,4608]{1,0:T(8,128)(2,1)} %get-tuple-element.74, bf16[4608,1024]{1,0:T(8,128)(2,1)} %copy-done.18), kind=kOutput, calls=%fused_computation.229 | convolution fusion | flops 7247757312 | bytes 19660800 | tf_op jit(solution)/shard_map/dot_general | solution.py:28
  479.4 15.2 %collective-permute-done.35 = bf16[2,2,2,144,1024]{4,3,2,1,0:T(8,128)(2,1)S(1)} collective-permute-done((bf16[2,2,2,144,1024]{4,3,2,1,0:T(8,128)(2,1)S(1)}, bf16[2,2,2,144,1024]{4,3,2,1,0:T(8,128)(2,1)S(1)}, u32[]{:S(2)}, u32[]{:S(2)}) %collective-permute-start.35) | collective-permute-done | bytes 2359328 | tf_op jit(solution)/shard_map/ppermute | solution.py:56
  497.2 6.3 fusion.1
  503.4 12.1 %fusion.68 = f32[768,1024]{1,0:T(8,128)S(1)} fusion(bf16[768,4608]{1,0:T(8,128)(2,1)} %get-tuple-element.78, bf16[4608,1024]{1,0:T(8,128)(2,1)} %get-tuple-element.154), kind=kOutput, calls=%fused_computation.230 | convolution fusion | flops 7247757312 | bytes 19660800 | tf_op jit(solution)/shard_map/dot_general | solution.py:28
  532.9 4.6 collective-permute-done.32
  538.0 3.9 multiply_reduce_fusion.2
  548.6 6.1 convolution_convert_fusion.3
  558.4 7.1 fusion.23
  568.7 16.0 %collective-permute-done.42 = f32[5,1024]{1,0:T(8,128)S(1)} collective-permute-done((f32[5,1024]{1,0:T(8,128)S(1)}, f32[5,1024]{1,0:T(8,128)S(1)}, u32[]{:S(2)}, u32[]{:S(2)}) %collective-permute-start.42) | collective-permute-done | bytes 20512 | tf_op jit(solution)/shard_map/ppermute | solution.py:56
  587.7 5.8 collective-permute-start.44
  597.6 4.4 fusion.20
  603.4 26.9 %collective-permute-done.36 = bf16[2,32,4608]{2,1,0:T(8,128)(2,1)S(1)} collective-permute-done((bf16[2,32,4608]{2,1,0:T(8,128)(2,1)S(1)}, bf16[2,32,4608]{2,1,0:T(8,128)(2,1)S(1)}, u32[]{:S(2)}, u32[]{:S(2)}) %collective-permute-start.36) | collective-permute-done | bytes 589856 | tf_op jit(solution)/shard_map/ppermute | solution.py:56
  641.3 3.9 collective-permute-done.49
  645.3 7.3 collective-permute-done.46
  652.7 13.9 %collective-permute-done.47 = bf16[2,144,1024]{2,1,0:T(8,128)(2,1)S(1)} collective-permute-done((bf16[2,144,1024]{2,1,0:T(8,128)(2,1)S(1)}, bf16[2,144,1024]{2,1,0:T(8,128)(2,1)S(1)}, u32[]{:S(2)}, u32[]{:S(2)}) %collective-permute-start.47) | collective-permute-done | bytes 589856 | tf_op jit(solution)/shard_map/ppermute | solution.py:56
  666.9 30.5 %collective-permute-done.48 = bf16[2,2,144,1024]{3,2,1,0:T(8,128)(2,1)S(1)} collective-permute-done((bf16[2,2,144,1024]{3,2,1,0:T(8,128)(2,1)S(1)}, bf16[2,2,144,1024]{3,2,1,0:T(8,128)(2,1)S(1)}, u32[]{:S(2)}, u32[]{:S(2)}) %collective-permute-start.48) | collective-permute-done | bytes 1179680 | tf_op jit(solution)/shard_map/ppermute | solution.py:56
  703.8 15.6 %collective-permute-done.54 = bf16[2,32,1024]{2,1,0:T(8,128)(2,1)S(1)} collective-permute-done((bf16[2,32,1024]{2,1,0:T(8,128)(2,1)S(1)}, bf16[2,32,1024]{2,1,0:T(8,128)(2,1)S(1)}, u32[]{:S(2)}, u32[]{:S(2)}) %collective-permute-start.54) | collective-permute-done | bytes 131104 | tf_op jit(solution)/shard_map/ppermute | solution.py:56
  720.8 11.5 %collective-permute-done.53 = bf16[2,144,1024]{2,1,0:T(8,128)(2,1)S(1)} collective-permute-done((bf16[2,144,1024]{2,1,0:T(8,128)(2,1)S(1)}, bf16[2,144,1024]{2,1,0:T(8,128)(2,1)S(1)}, u32[]{:S(2)}, u32[]{:S(2)}) %collective-permute-start.53) | collective-permute-done | bytes 589856 | tf_op jit(solution)/shard_map/ppermute | solution.py:56
  736.3 11.3 %collective-permute-done.58 = bf16[144,1024]{1,0:T(8,128)(2,1)S(1)} collective-permute-done((bf16[144,1024]{1,0:T(8,128)(2,1)S(1)}, bf16[144,1024]{1,0:T(8,128)(2,1)S(1)}, u32[]{:S(2)}, u32[]{:S(2)}) %collective-permute-start.58) | collective-permute-done | bytes 294944 | tf_op jit(solution)/shard_map/ppermute | solution.py:56
  747.8 5.1 collective-permute-done.60
  757.1 10.6 %fusion.44 = bf16[1,768,1024]{2,1,0:T(8,128)(2,1)} fusion(f32[768,1024]{1,0:T(8,128)S(1)} %copy-done.6, bf16[768,4608]{1,0:T(8,128)(2,1)} %get-tuple-element.93, bf16[1024,4608]{1,0:T(8,128)(2,1)S(1)} %bitcast.274), kind=kOutput, calls=%fused_computation.119 | convolution fusion | flops 7249330176 | bytes 21233664 | tf_op jit(solution)/shard_map/dot_general | solution.py:16
  778.4 12.5 %collective-permute-done.62 = bf16[2,144,1024]{2,1,0:T(8,128)(2,1)S(1)} collective-permute-done((bf16[2,144,1024]{2,1,0:T(8,128)(2,1)S(1)}, bf16[2,144,1024]{2,1,0:T(8,128)(2,1)S(1)}, u32[]{:S(2)}, u32[]{:S(2)}) %collective-permute-start.62) | collective-permute-done | bytes 589856 | tf_op jit(solution)/shard_map/ppermute | solution.py:56
  799.1 9.9 %collective-permute-done.67 = bf16[2,144,1024]{2,1,0:T(8,128)(2,1)S(1)} collective-permute-done((bf16[2,144,1024]{2,1,0:T(8,128)(2,1)S(1)}, bf16[2,144,1024]{2,1,0:T(8,128)(2,1)S(1)}, u32[]{:S(2)}, u32[]{:S(2)}) %collective-permute-start.67) | collective-permute-done | bytes 589856 | tf_op jit(solution)/shard_map/ppermute | solution.py:56
  (422 shorter events, 193.9 us)
Async XLA Ops:
  2.3 31.4 %collective-permute-start.13 = (bf16[144,1024]{1,0:T(8,128)(2,1)S(1)}, bf16[144,1024]{1,0:T(8,128)(2,1)S(1)}, u32[]{:S(2)}, u32[]{:S(2)}) collective-permute-start(bf16[144,1024]{1,0:T(8,128)(2,1)S(1)} %constant_dynamic-slice_fusion.4), channel_id=1, source_target_pairs={{0,8},{8,0},{16,24},{24,16},{1,9},{9,1},{17,25},{25,17},{2,10},{10... | collective-permute-start | bytes 884744 | tf_op jit(solution)/shard_map/ppermute | solution.py:56
  5.5 28.3 %collective-permute-start.18 = (bf16[144,1024]{1,0:T(8,128)(2,1)S(1)}, bf16[144,1024]{1,0:T(8,128)(2,1)S(1)}, u32[]{:S(2)}, u32[]{:S(2)}) collective-permute-start(bf16[144,1024]{1,0:T(8,128)(2,1)S(1)} %constant_dynamic-slice_fusion.3), channel_id=1, source_target_pairs={{0,8},{8,0},{16,24},{24,16},{1,9},{9,1},{17,25},{25,17},{2,10},{10... | collective-permute-start | bytes 884744 | tf_op jit(solution)/shard_map/ppermute | solution.py:56
  6.5 22.5 %collective-permute-start.2 = (bf16[96,1024]{1,0:T(8,128)(2,1)S(1)}, bf16[96,1024]{1,0:T(8,128)(2,1)S(1)}, u32[]{:S(2)}, u32[]{:S(2)}) collective-permute-start(bf16[96,1024]{1,0:T(8,128)(2,1)S(1)} %constant_dynamic-slice_fusion.6), channel_id=1, source_target_pairs={{0,8},{8,0},{16,24},{24,16},{1,9},{9,1},{17,25},{25,17},{2,10},{10... | collective-permute-start | bytes 589832 | tf_op jit(solution)/shard_map/ppermute | solution.py:56
  25.4 40.7 %collective-permute-start.23 = (bf16[32,4608]{1,0:T(8,128)(2,1)S(1)}, bf16[32,4608]{1,0:T(8,128)(2,1)S(1)}, u32[]{:S(2)}, u32[]{:S(2)}) collective-permute-start(bf16[32,4608]{1,0:T(8,128)(2,1)S(1)} %constant_dynamic-slice_fusion.2), channel_id=1, source_target_pairs={{0,8},{8,0},{16,24},{24,16},{1,9},{9,1},{17,25},{25,17},{2,10},{10... | collective-permute-start | bytes 884744 | tf_op jit(solution)/shard_map/ppermute | solution.py:56
  29.2 35.4 %collective-permute-start.3 = (bf16[2,96,1024]{2,1,0:T(8,128)(2,1)S(1)}, bf16[2,96,1024]{2,1,0:T(8,128)(2,1)S(1)}, u32[]{:S(2)}, u32[]{:S(2)}) collective-permute-start(bf16[2,96,1024]{2,1,0:T(8,128)(2,1)S(1)} %broadcast_select_fusion.31), channel_id=1, source_target_pairs={{0,16},{8,24},{16,0},{24,8},{1,17},{9,25},{17,1},{25,9},{2,18},{10... | collective-permute-start | bytes 1179656 | tf_op jit(solution)/shard_map/ppermute | solution.py:56
  32.5 33.8 %collective-permute-start.10 = (bf16[2,2,32,1024]{3,2,1,0:T(8,128)(2,1)S(1)}, bf16[2,2,32,1024]{3,2,1,0:T(8,128)(2,1)S(1)}, u32[]{:S(2)}, u32[]{:S(2)}) collective-permute-start(bf16[2,2,32,1024]{3,2,1,0:T(8,128)(2,1)S(1)} %broadcast_select_fusion.33), channel_id=1, source_target_pairs={{0,2},{1,3},{2,0},{3,1},{4,6},{5,7},{6,4},{7,5},{8,10},{9,11},{10,... | collective-permute-start | bytes 786440 | tf_op jit(solution)/shard_map/ppermute | solution.py:56
  33.9 43.2 %collective-permute-start.14 = (bf16[2,144,1024]{2,1,0:T(8,128)(2,1)S(1)}, bf16[2,144,1024]{2,1,0:T(8,128)(2,1)S(1)}, u32[]{:S(2)}, u32[]{:S(2)}) collective-permute-start(bf16[2,144,1024]{2,1,0:T(8,128)(2,1)S(1)} %get-tuple-element.169), channel_id=1, source_target_pairs={{0,16},{8,24},{16,0},{24,8},{1,17},{9,25},{17,1},{25,9},{2,18},{10... | collective-permute-start | bytes 1769480 | tf_op jit(solution)/shard_map/ppermute | solution.py:56
  36.8 53.0 %collective-permute-start.19 = (bf16[2,144,1024]{2,1,0:T(8,128)(2,1)S(1)}, bf16[2,144,1024]{2,1,0:T(8,128)(2,1)S(1)}, u32[]{:S(2)}, u32[]{:S(2)}) collective-permute-start(bf16[2,144,1024]{2,1,0:T(8,128)(2,1)S(1)} %get-tuple-element.168), channel_id=1, source_target_pairs={{0,16},{8,24},{16,0},{24,8},{1,17},{9,25},{17,1},{25,9},{2,18},{10... | collective-permute-start | bytes 1769480 | tf_op jit(solution)/shard_map/ppermute | solution.py:56
  64.7 28.0 %collective-permute-start.4 = (bf16[2,2,96,1024]{3,2,1,0:T(8,128)(2,1)S(1)}, bf16[2,2,96,1024]{3,2,1,0:T(8,128)(2,1)S(1)}, u32[]{:S(2)}, u32[]{:S(2)}) collective-permute-start(bf16[2,2,96,1024]{3,2,1,0:T(8,128)(2,1)S(1)} %broadcast_select_fusion.21), channel_id=1, source_target_pairs={{0,4},{1,5},{2,6},{3,7},{4,0},{5,1},{6,2},{7,3},{8,12},{9,13},{10,... | collective-permute-start | bytes 2359304 | tf_op jit(solution)/shard_map/ppermute | solution.py:56
  66.2 61.6 %collective-permute-start.24 = (bf16[2,32,4608]{2,1,0:T(8,128)(2,1)S(1)}, bf16[2,32,4608]{2,1,0:T(8,128)(2,1)S(1)}, u32[]{:S(2)}, u32[]{:S(2)}) collective-permute-start(bf16[2,32,4608]{2,1,0:T(8,128)(2,1)S(1)} %broadcast_select_fusion.25), channel_id=1, source_target_pairs={{0,16},{8,24},{16,0},{24,8},{1,17},{9,25},{17,1},{25,9},{2,18},{10... | collective-permute-start | bytes 1769480 | tf_op jit(solution)/shard_map/ppermute | solution.py:56
  66.4 62.9 %collective-permute-start.11 = (bf16[2,2,2,32,1024]{4,3,2,1,0:T(8,128)(2,1)S(1)}, bf16[2,2,2,32,1024]{4,3,2,1,0:T(8,128)(2,1)S(1)}, u32[]{:S(2)}, u32[]{:S(2)}) collective-permute-start(bf16[2,2,2,32,1024]{4,3,2,1,0:T(8,128)(2,1)S(1)} %broadcast_select_fusion.29), channel_id=1, source_target_pairs={{0,4},{1,5},{2,6},{3,7},{4,0},{5,1},{6,2},{7,3},{8,12},{9,13},{10,... | collective-permute-start | bytes 1572872 | tf_op jit(solution)/shard_map/ppermute | solution.py:56
  90.2 42.0 %collective-permute-start.15 = (bf16[2,2,144,1024]{3,2,1,0:T(8,128)(2,1)S(1)}, bf16[2,2,144,1024]{3,2,1,0:T(8,128)(2,1)S(1)}, u32[]{:S(2)}, u32[]{:S(2)}) collective-permute-start(bf16[2,2,144,1024]{3,2,1,0:T(8,128)(2,1)S(1)} %get-tuple-element.167), channel_id=1, source_target_pairs={{0,4},{1,5},{2,6},{3,7},{4,0},{5,1},{6,2},{7,3},{8,12},{9,13},{10,... | collective-permute-start | bytes 3538952 | tf_op jit(solution)/shard_map/ppermute | solution.py:56
  91.5 86.7 %collective-permute-start.20 = (bf16[2,2,144,1024]{3,2,1,0:T(8,128)(2,1)S(1)}, bf16[2,2,144,1024]{3,2,1,0:T(8,128)(2,1)S(1)}, u32[]{:S(2)}, u32[]{:S(2)}) collective-permute-start(bf16[2,2,144,1024]{3,2,1,0:T(8,128)(2,1)S(1)} %get-tuple-element.166), channel_id=1, source_target_pairs={{0,2},{1,3},{2,0},{3,1},{4,6},{5,7},{6,4},{7,5},{8,10},{9,11},{10,... | collective-permute-start | bytes 3538952 | tf_op jit(solution)/shard_map/ppermute | solution.py:56
  92.9 39.8 %collective-permute-start.5 = (bf16[2,2,2,96,1024]{4,3,2,1,0:T(8,128)(2,1)S(1)}, bf16[2,2,2,96,1024]{4,3,2,1,0:T(8,128)(2,1)S(1)}, u32[]{:S(2)}, u32[]{:S(2)}) collective-permute-start(bf16[2,2,2,96,1024]{4,3,2,1,0:T(8,128)(2,1)S(1)} %broadcast_select_fusion.12), channel_id=1, source_target_pairs={{0,2},{1,3},{2,0},{3,1},{4,6},{5,7},{6,4},{7,5},{8,10},{9,11},{10,... | collective-permute-start | bytes 4718600 | tf_op jit(solution)/shard_map/ppermute | solution.py:56
  127.9 52.2 %collective-permute-start.25 = (bf16[2,2,32,4608]{3,2,1,0:T(8,128)(2,1)S(1)}, bf16[2,2,32,4608]{3,2,1,0:T(8,128)(2,1)S(1)}, u32[]{:S(2)}, u32[]{:S(2)}) collective-permute-start(bf16[2,2,32,4608]{3,2,1,0:T(8,128)(2,1)S(1)} %broadcast_select_fusion.16), channel_id=1, source_target_pairs={{0,2},{1,3},{2,0},{3,1},{4,6},{5,7},{6,4},{7,5},{8,10},{9,11},{10,... | collective-permute-start | bytes 3538952 | tf_op jit(solution)/shard_map/ppermute | solution.py:56
  129.4 49.2 %collective-permute-start.12 = (bf16[2,2,2,2,32,1024]{5,4,3,2,1,0:T(8,128)(2,1)S(1)}, bf16[2,2,2,2,32,1024]{5,4,3,2,1,0:T(8,128)(2,1)S(1)}, u32[]{:S(2)}, u32[]{:S(2)}) collective-permute-start(bf16[2,2,2,2,32,1024]{5,4,3,2,1,0:T(8,128)(2,1)S(1)} %broadcast_select_fusion.19), channel_id=1, source_target_pairs={{0,1},{1,0},{2,3},{3,2},{4,5},{5,4},{6,7},{7,6},{8,9},{9,8},{10,11... | collective-permute-start | bytes 3145736 | tf_op jit(solution)/shard_map/ppermute | solution.py:56
  132.4 74.3 %collective-permute-start.16 = (bf16[2,2,2,144,1024]{4,3,2,1,0:T(8,128)(2,1)S(1)}, bf16[2,2,2,144,1024]{4,3,2,1,0:T(8,128)(2,1)S(1)}, u32[]{:S(2)}, u32[]{:S(2)}) collective-permute-start(bf16[2,2,2,144,1024]{4,3,2,1,0:T(8,128)(2,1)S(1)} %broadcast_select_fusion.10), channel_id=1, source_target_pairs={{0,2},{1,3},{2,0},{3,1},{4,6},{5,7},{6,4},{7,5},{8,10},{9,11},{10,... | collective-permute-start | bytes 7077896 | tf_op jit(solution)/shard_map/ppermute | solution.py:56
  133.0 104.3 %collective-permute-start.6 = (bf16[2,2,2,2,96,1024]{5,4,3,2,1,0:T(8,128)(2,1)S(1)}, bf16[2,2,2,2,96,1024]{5,4,3,2,1,0:T(8,128)(2,1)S(1)}, u32[]{:S(2)}, u32[]{:S(2)}) collective-permute-start(bf16[2,2,2,2,96,1024]{5,4,3,2,1,0:T(8,128)(2,1)S(1)} %broadcast_select_fusion.4), channel_id=1, source_target_pairs={{0,1},{1,0},{2,3},{3,2},{4,5},{5,4},{6,7},{7,6},{8,9},{9,8},{10,11... | collective-permute-start | bytes 9437192 | tf_op jit(solution)/shard_map/ppermute | solution.py:56
  178.4 54.5 %collective-permute-start.21 = (bf16[2,2,2,144,1024]{4,3,2,1,0:T(8,128)(2,1)S(1)}, bf16[2,2,2,144,1024]{4,3,2,1,0:T(8,128)(2,1)}, u32[]{:S(2)}, u32[]{:S(2)}) collective-permute-start(bf16[2,2,2,144,1024]{4,3,2,1,0:T(8,128)(2,1)S(1)} %broadcast_select_fusion.9), channel_id=1, source_target_pairs={{0,4},{1,5},{2,6},{3,7},{4,0},{5,1},{6,2},{7,3},{8,12},{9,13},{10,... | collective-permute-start | bytes 7077896 | tf_op jit(solution)/shard_map/ppermute | solution.py:56
  181.8 100.2 %collective-permute-start.26 = (bf16[2,2,2,32,4608]{4,3,2,1,0:T(8,128)(2,1)}, bf16[2,2,2,32,4608]{4,3,2,1,0:T(8,128)(2,1)}, u32[]{:S(2)}, u32[]{:S(2)}) collective-permute-start(bf16[2,2,2,32,4608]{4,3,2,1,0:T(8,128)(2,1)} %broadcast_select_fusion.8), channel_id=1, source_target_pairs={{0,4},{1,5},{2,6},{3,7},{4,0},{5,1},{6,2},{7,3},{8,12},{9,13},{10,... | collective-permute-start | bytes 7077896 | tf_op jit(solution)/shard_map/ppermute | solution.py:56
  209.3 87.7 %collective-permute-start.17 = (bf16[2,2,2,2,144,1024]{5,4,3,2,1,0:T(8,128)(2,1)}, bf16[2,2,2,2,144,1024]{5,4,3,2,1,0:T(8,128)(2,1)}, u32[]{:S(2)}, u32[]{:S(2)}) collective-permute-start(bf16[2,2,2,2,144,1024]{5,4,3,2,1,0:T(8,128)(2,1)} %broadcast_select_fusion.3), channel_id=1, source_target_pairs={{0,1},{1,0},{2,3},{3,2},{4,5},{5,4},{6,7},{7,6},{8,9},{9,8},{10,11... | collective-permute-start | bytes 14155784 | tf_op jit(solution)/shard_map/ppermute | solution.py:56
  237.3 59.8 %collective-permute-start.22 = (bf16[2,2,2,2,144,1024]{5,4,3,2,1,0:T(8,128)(2,1)}, bf16[2,2,2,2,144,1024]{5,4,3,2,1,0:T(8,128)(2,1)}, u32[]{:S(2)}, u32[]{:S(2)}) collective-permute-start(bf16[2,2,2,2,144,1024]{5,4,3,2,1,0:T(8,128)(2,1)} %broadcast_select_fusion.2), channel_id=1, source_target_pairs={{0,1},{1,0},{2,3},{3,2},{4,5},{5,4},{6,7},{7,6},{8,9},{9,8},{10,11... | collective-permute-start | bytes 14155784 | tf_op jit(solution)/shard_map/ppermute | solution.py:56
  249.1 38.8 %collective-permute-start.7 = (bf16[2,1024]{1,0:T(2,128)(2,1)S(1)}, bf16[2,1024]{1,0:T(2,128)(2,1)S(1)}, u32[]{:S(2)}, u32[]{:S(2)}) collective-permute-start(bf16[2,1024]{1,0:T(2,128)(2,1)S(1)} %slice.112), channel_id=1, source_target_pairs={{0,8},{8,16},{16,24},{1,9},{9,17},{17,25},{2,10},{10,18},{18,26},{... | collective-permute-start | bytes 12296 | tf_op jit(solution)/shard_map/ppermute | solution.py:12
  287.0 67.8 %collective-permute-start.27 = (bf16[2,2,2,2,32,4608]{5,4,3,2,1,0:T(8,128)(2,1)}, bf16[2,2,2,2,32,4608]{5,4,3,2,1,0:T(8,128)(2,1)}, u32[]{:S(2)}, u32[]{:S(2)}) collective-permute-start(bf16[2,2,2,2,32,4608]{5,4,3,2,1,0:T(8,128)(2,1)} %broadcast_select_fusion.1), channel_id=1, source_target_pairs={{0,1},{1,0},{2,3},{3,2},{4,5},{5,4},{6,7},{7,6},{8,9},{9,8},{10,11... | collective-permute-start | bytes 14155784 | tf_op jit(solution)/shard_map/ppermute | solution.py:56
  354.8 30.4 %collective-permute-start.28 = (bf16[2,2,2,2,32,4608]{5,4,3,2,1,0:T(8,128)(2,1)}, bf16[2,2,2,2,32,4608]{5,4,3,2,1,0:T(8,128)(2,1)}, u32[]{:S(2)}, u32[]{:S(2)}) collective-permute-start(bf16[2,2,2,2,32,4608]{5,4,3,2,1,0:T(8,128)(2,1)} %dynamic-slice_bitcast_fusion.2), channel_id=1, source_target_pairs={{0,1},{1,0},{2,3},{3,2},{4,5},{5,4},{6,7},{7,6},{8,9},{9,8},{10,11... | collective-permute-start | bytes 14155784 | tf_op jit(solution)/shard_map/ppermute | solution.py:56
  409.9 53.2 %collective-permute-start.31 = (bf16[2,2,2,32,4608]{4,3,2,1,0:T(8,128)(2,1)}, bf16[2,2,2,32,4608]{4,3,2,1,0:T(8,128)(2,1)}, u32[]{:S(2)}, u32[]{:S(2)}) collective-permute-start(bf16[2,2,2,32,4608]{4,3,2,1,0:T(8,128)(2,1)} %dynamic-slice_bitcast_fusion.6), channel_id=1, source_target_pairs={{0,2},{1,3},{2,0},{3,1},{4,6},{5,7},{6,4},{7,5},{8,10},{9,11},{10,... | collective-permute-start | bytes 7077896 | tf_op jit(solution)/shard_map/ppermute | solution.py:56
  434.8 62.3 %collective-permute-start.30 = (bf16[2,2,2,2,144,1024]{5,4,3,2,1,0:T(8,128)(2,1)}, bf16[2,2,2,2,144,1024]{5,4,3,2,1,0:T(8,128)(2,1)}, u32[]{:S(2)}, u32[]{:S(2)}) collective-permute-start(bf16[2,2,2,2,144,1024]{5,4,3,2,1,0:T(8,128)(2,1)} %dynamic-slice_bitcast_fusion), channel_id=1, source_target_pairs={{0,1},{1,0},{2,3},{3,2},{4,5},{5,4},{6,7},{7,6},{8,9},{9,8},{10,11... | collective-permute-start | bytes 14155784 | tf_op jit(solution)/shard_map/ppermute | solution.py:56
  442.1 52.5 %collective-permute-start.35 = (bf16[2,2,2,144,1024]{4,3,2,1,0:T(8,128)(2,1)S(1)}, bf16[2,2,2,144,1024]{4,3,2,1,0:T(8,128)(2,1)S(1)}, u32[]{:S(2)}, u32[]{:S(2)}) collective-permute-start(bf16[2,2,2,144,1024]{4,3,2,1,0:T(8,128)(2,1)S(1)} %dynamic-slice_bitcast_fusion.5), channel_id=1, source_target_pairs={{0,4},{1,5},{2,6},{3,7},{4,0},{5,1},{6,2},{7,3},{8,12},{9,13},{10,... | collective-permute-start | bytes 7077896 | tf_op jit(solution)/shard_map/ppermute | solution.py:56
  517.5 29.3 %collective-permute-start.34 = (bf16[2,2,32,4608]{3,2,1,0:T(8,128)(2,1)}, bf16[2,2,32,4608]{3,2,1,0:T(8,128)(2,1)}, u32[]{:S(2)}, u32[]{:S(2)}) collective-permute-start(bf16[2,2,32,4608]{3,2,1,0:T(8,128)(2,1)} %dynamic-slice_bitcast_fusion.10), channel_id=1, source_target_pairs={{0,4},{1,5},{2,6},{3,7},{4,0},{5,1},{6,2},{7,3},{8,12},{9,13},{10,... | collective-permute-start | bytes 3538952 | tf_op jit(solution)/shard_map/ppermute | solution.py:56
  524.1 19.6 %collective-permute-start.33 = (bf16[2,2,2,2,32,1024]{5,4,3,2,1,0:T(8,128)(2,1)}, bf16[2,2,2,2,32,1024]{5,4,3,2,1,0:T(8,128)(2,1)}, u32[]{:S(2)}, u32[]{:S(2)}) collective-permute-start(bf16[2,2,2,2,32,1024]{5,4,3,2,1,0:T(8,128)(2,1)} %dynamic-slice_bitcast_fusion.11), channel_id=1, source_target_pairs={{0,1},{1,0},{2,3},{3,2},{4,5},{5,4},{6,7},{7,6},{8,9},{9,8},{10,11... | collective-permute-start | bytes 3145736 | tf_op jit(solution)/shard_map/ppermute | solution.py:56
  532.1 98.4 %collective-permute-start.38 = (bf16[2,2,2,144,1024]{4,3,2,1,0:T(8,128)(2,1)}, bf16[2,2,2,144,1024]{4,3,2,1,0:T(8,128)(2,1)}, u32[]{:S(2)}, u32[]{:S(2)}) collective-permute-start(bf16[2,2,2,144,1024]{4,3,2,1,0:T(8,128)(2,1)} %dynamic-slice_bitcast_fusion.4), channel_id=1, source_target_pairs={{0,2},{1,3},{2,0},{3,1},{4,6},{5,7},{6,4},{7,5},{8,10},{9,11},{10,... | collective-permute-start | bytes 7077896 | tf_op jit(solution)/shard_map/ppermute | solution.py:56
  556.7 77.1 %collective-permute-start.40 = (bf16[2,2,2,2,96,1024]{5,4,3,2,1,0:T(8,128)(2,1)}, bf16[2,2,2,2,96,1024]{5,4,3,2,1,0:T(8,128)(2,1)}, u32[]{:S(2)}, u32[]{:S(2)}) collective-permute-start(bf16[2,2,2,2,96,1024]{5,4,3,2,1,0:T(8,128)(2,1)} %dynamic-slice_bitcast_fusion.3), channel_id=1, source_target_pairs={{0,1},{1,0},{2,3},{3,2},{4,5},{5,4},{6,7},{7,6},{8,9},{9,8},{10,11... | collective-permute-start | bytes 9437192 | tf_op jit(solution)/shard_map/ppermute | solution.py:56
  565.7 37.5 %collective-permute-start.39 = (bf16[2,2,2,32,1024]{4,3,2,1,0:T(8,128)(2,1)S(1)}, bf16[2,2,2,32,1024]{4,3,2,1,0:T(8,128)(2,1)S(1)}, u32[]{:S(2)}, u32[]{:S(2)}) collective-permute-start(bf16[2,2,2,32,1024]{4,3,2,1,0:T(8,128)(2,1)S(1)} %dynamic-slice_bitcast_fusion.16), channel_id=1, source_target_pairs={{0,4},{1,5},{2,6},{3,7},{4,0},{5,1},{6,2},{7,3},{8,12},{9,13},{10,... | collective-permute-start | bytes 1572872 | tf_op jit(solution)/shard_map/ppermute | solution.py:56
  567.0 17.6 %collective-permute-start.42 = (f32[5,1024]{1,0:T(8,128)S(1)}, f32[5,1024]{1,0:T(8,128)S(1)}, u32[]{:S(2)}, u32[]{:S(2)}) collective-permute-start(f32[5,1024]{1,0:T(8,128)S(1)} %fusion.59), channel_id=1, source_target_pairs={{0,2},{1,3},{2,0},{3,1},{4,6},{5,7},{6,4},{7,5},{8,10},{9,11},{10,... | collective-permute-start | bytes 61448 | tf_op jit(solution)/shard_map/ppermute | solution.py:56
  567.5 65.7 %collective-permute-start.37 = (bf16[2,2,144,1024]{3,2,1,0:T(8,128)(2,1)S(1)}, bf16[2,2,144,1024]{3,2,1,0:T(8,128)(2,1)S(1)}, u32[]{:S(2)}, u32[]{:S(2)}) collective-permute-start(bf16[2,2,144,1024]{3,2,1,0:T(8,128)(2,1)S(1)} %dynamic-slice_bitcast_fusion.9), channel_id=1, source_target_pairs={{0,2},{1,3},{2,0},{3,1},{4,6},{5,7},{6,4},{7,5},{8,10},{9,11},{10,... | collective-permute-start | bytes 3538952 | tf_op jit(solution)/shard_map/ppermute | solution.py:56
  602.0 28.3 %collective-permute-start.36 = (bf16[2,32,4608]{2,1,0:T(8,128)(2,1)S(1)}, bf16[2,32,4608]{2,1,0:T(8,128)(2,1)S(1)}, u32[]{:S(2)}, u32[]{:S(2)}) collective-permute-start(bf16[2,32,4608]{2,1,0:T(8,128)(2,1)S(1)} %dynamic-slice_bitcast_fusion.15), channel_id=1, source_target_pairs={{0,16},{8,24},{16,0},{24,8},{1,17},{9,25},{17,1},{25,9},{2,18},{10... | collective-permute-start | bytes 1769480 | tf_op jit(solution)/shard_map/ppermute | solution.py:56
  637.4 60.4 %collective-permute-start.50 = (bf16[2,2,2,96,1024]{4,3,2,1,0:T(8,128)(2,1)S(1)}, bf16[2,2,2,96,1024]{4,3,2,1,0:T(8,128)(2,1)S(1)}, u32[]{:S(2)}, u32[]{:S(2)}) collective-permute-start(bf16[2,2,2,96,1024]{4,3,2,1,0:T(8,128)(2,1)S(1)} %dynamic-slice_bitcast_fusion.7), channel_id=1, source_target_pairs={{0,4},{1,5},{2,6},{3,7},{4,0},{5,1},{6,2},{7,3},{8,12},{9,13},{10,... | collective-permute-start | bytes 4718600 | tf_op jit(solution)/shard_map/ppermute | solution.py:56
  639.7 57.7 %collective-permute-start.48 = (bf16[2,2,144,1024]{3,2,1,0:T(8,128)(2,1)S(1)}, bf16[2,2,144,1024]{3,2,1,0:T(8,128)(2,1)S(1)}, u32[]{:S(2)}, u32[]{:S(2)}) collective-permute-start(bf16[2,2,144,1024]{3,2,1,0:T(8,128)(2,1)S(1)} %dynamic-slice_bitcast_fusion.8), channel_id=1, source_target_pairs={{0,4},{1,5},{2,6},{3,7},{4,0},{5,1},{6,2},{7,3},{8,12},{9,13},{10,... | collective-permute-start | bytes 3538952 | tf_op jit(solution)/shard_map/ppermute | solution.py:56
  640.0 26.7 %collective-permute-start.47 = (bf16[2,144,1024]{2,1,0:T(8,128)(2,1)S(1)}, bf16[2,144,1024]{2,1,0:T(8,128)(2,1)S(1)}, u32[]{:S(2)}, u32[]{:S(2)}) collective-permute-start(bf16[2,144,1024]{2,1,0:T(8,128)(2,1)S(1)} %dynamic-slice_bitcast_fusion.14), channel_id=1, source_target_pairs={{0,16},{8,24},{16,0},{24,8},{1,17},{9,25},{17,1},{25,9},{2,18},{10... | collective-permute-start | bytes 1769480 | tf_op jit(solution)/shard_map/ppermute | solution.py:56
  698.9 33.7 %collective-permute-start.55 = (bf16[2,2,96,1024]{3,2,1,0:T(8,128)(2,1)S(1)}, bf16[2,2,96,1024]{3,2,1,0:T(8,128)(2,1)S(1)}, u32[]{:S(2)}, u32[]{:S(2)}) collective-permute-start(bf16[2,2,96,1024]{3,2,1,0:T(8,128)(2,1)S(1)} %dynamic-slice_bitcast_fusion.12), channel_id=1, source_target_pairs={{0,2},{1,3},{2,0},{3,1},{4,6},{5,7},{6,4},{7,5},{8,10},{9,11},{10,... | collective-permute-start | bytes 2359304 | tf_op jit(solution)/shard_map/ppermute | solution.py:56
  699.3 20.1 %collective-permute-start.54 = (bf16[2,32,1024]{2,1,0:T(8,128)(2,1)S(1)}, bf16[2,32,1024]{2,1,0:T(8,128)(2,1)S(1)}, u32[]{:S(2)}, u32[]{:S(2)}) collective-permute-start(bf16[2,32,1024]{2,1,0:T(8,128)(2,1)S(1)} %dynamic-slice_bitcast_fusion.23), channel_id=1, source_target_pairs={{0,16},{8,24},{16,0},{24,8},{1,17},{9,25},{17,1},{25,9},{2,18},{10... | collective-permute-start | bytes 393224 | tf_op jit(solution)/shard_map/ppermute | solution.py:56
  699.5 32.9 %collective-permute-start.53 = (bf16[2,144,1024]{2,1,0:T(8,128)(2,1)S(1)}, bf16[2,144,1024]{2,1,0:T(8,128)(2,1)S(1)}, u32[]{:S(2)}, u32[]{:S(2)}) collective-permute-start(bf16[2,144,1024]{2,1,0:T(8,128)(2,1)S(1)} %dynamic-slice_bitcast_fusion.13), channel_id=1, source_target_pairs={{0,16},{8,24},{16,0},{24,8},{1,17},{9,25},{17,1},{25,9},{2,18},{10... | collective-permute-start | bytes 1769480 | tf_op jit(solution)/shard_map/ppermute | solution.py:56
  701.9 17.6 %collective-permute-start.51 = (bf16[32,4608]{1,0:T(8,128)(2,1)S(1)}, bf16[32,4608]{1,0:T(8,128)(2,1)S(1)}, u32[]{:S(2)}, u32[]{:S(2)}) collective-permute-start(bf16[32,4608]{1,0:T(8,128)(2,1)S(1)} %fusion.52), channel_id=1, source_target_pairs={{0,4},{1,5},{2,6},{3,7},{4,0},{5,1},{6,2},{7,3},{8,12},{9,13},{10,... | collective-permute-start | bytes 884744 | tf_op jit(solution)/shard_map/ppermute | solution.py:56
  703.7 17.0 %collective-permute-start.52 = (bf16[144,1024]{1,0:T(8,128)(2,1)S(1)}, bf16[144,1024]{1,0:T(8,128)(2,1)S(1)}, u32[]{:S(2)}, u32[]{:S(2)}) collective-permute-start(bf16[144,1024]{1,0:T(8,128)(2,1)S(1)} %dynamic-slice_bitcast_fusion.19), channel_id=1, source_target_pairs={{0,8},{8,0},{16,24},{24,16},{1,9},{9,1},{17,25},{25,17},{2,10},{10... | collective-permute-start | bytes 884744 | tf_op jit(solution)/shard_map/ppermute | solution.py:56
  734.6 18.3 %collective-permute-start.60 = (bf16[2,96,1024]{2,1,0:T(8,128)(2,1)S(1)}, bf16[2,96,1024]{2,1,0:T(8,128)(2,1)S(1)}, u32[]{:S(2)}, u32[]{:S(2)}) collective-permute-start(bf16[2,96,1024]{2,1,0:T(8,128)(2,1)S(1)} %dynamic-slice_bitcast_fusion.17), channel_id=1, source_target_pairs={{0,16},{8,24},{16,0},{24,8},{1,17},{9,25},{17,1},{25,9},{2,18},{10... | collective-permute-start | bytes 1179656 | tf_op jit(solution)/shard_map/ppermute | solution.py:56
  735.9 17.8 %collective-permute-start.56 = (bf16[2,32,4608]{2,1,0:T(8,128)(2,1)S(1)}, bf16[2,32,4608]{2,1,0:T(8,128)(2,1)S(1)}, u32[]{:S(2)}, u32[]{:S(2)}) collective-permute-start(bf16[2,32,4608]{2,1,0:T(8,128)(2,1)S(1)} %broadcast_select_fusion.24), channel_id=1, source_target_pairs={{0,2},{1,3},{2,0},{3,1},{4,6},{5,7},{6,4},{7,5},{8,10},{9,11},{10,... | collective-permute-start | bytes 1769480 | tf_op jit(solution)/shard_map/ppermute | solution.py:56
  753.9 37.2 %collective-permute-start.61 = (bf16[2,2,32,4608]{3,2,1,0:T(8,128)(2,1)S(1)}, bf16[2,2,32,4608]{3,2,1,0:T(8,128)(2,1)S(1)}, u32[]{:S(2)}, u32[]{:S(2)}) collective-permute-start(bf16[2,2,32,4608]{3,2,1,0:T(8,128)(2,1)S(1)} %broadcast_select_fusion.15), channel_id=1, source_target_pairs={{0,1},{1,0},{2,3},{3,2},{4,5},{5,4},{6,7},{7,6},{8,9},{9,8},{10,11... | collective-permute-start | bytes 3538952 | tf_op jit(solution)/shard_map/ppermute | solution.py:56
  771.1 19.8 %collective-permute-start.62 = (bf16[2,144,1024]{2,1,0:T(8,128)(2,1)S(1)}, bf16[2,144,1024]{2,1,0:T(8,128)(2,1)S(1)}, u32[]{:S(2)}, u32[]{:S(2)}) collective-permute-start(bf16[2,144,1024]{2,1,0:T(8,128)(2,1)S(1)} %broadcast_select_fusion.23), channel_id=1, source_target_pairs={{0,4},{1,5},{2,6},{3,7},{4,0},{5,1},{6,2},{7,3},{8,12},{9,13},{10,... | collective-permute-start | bytes 1769480 | tf_op jit(solution)/shard_map/ppermute | solution.py:56
  (100 other events, 3065.6 us)

commit v2 on v1

--- a/solution.py
+++ b/solution.py
@@ -98,51 +98,136 @@
     return block
 
 
-def gather_rows(block, order):
-    replicas = lax.axis_size("replica")
-    rows = block.shape[0] // replicas
-    piece = lax.dynamic_slice_in_dim(block, lax.axis_index("replica") * rows, rows, 0)
-    whole = spread(piece, shard_route() + route(order) + CORE, [])
-    return whole.reshape((-1, block.shape[1]))
+def halved(value):
+    half = value.shape[-2] // 2
+    return [value[..., :half, :], value[..., half:, :]]
+
+
+def joined(parts):
+    return jnp.concatenate(parts, axis=-2)
+
+
+class Gather:
+    def __init__(self, block):
+        replicas = lax.axis_size("replica")
+        rows = block.shape[0] // replicas
+        self.value = lax.dynamic_slice_in_dim(
+            block, lax.axis_index("replica") * rows, rows, 0
+        )
+        self.width = block.shape[1]
+        self.held = []
+        self.near, self.orders, self.last = shard_route(), [route(0), route(1)], CORE
+        self.parts = None
+
+    def live(self):
+        return bool(self.near or self.orders[0] or self.last)
+
+    def step(self):
+        if self.near:
+            hop = self.near.pop(0)
+            self.value = spread(self.value, [hop], self.held)
+            self.held.append(hop)
+        elif self.orders[0]:
+            if self.parts is None:
+                self.parts = [(part, list(self.held)) for part in halved(self.value)]
+            moved = []
+            for (part, held), order in zip(self.parts, self.orders):
+                hop = order.pop(0)
+                moved.append((spread(part, [hop], held), held + [hop]))
+            self.parts = moved
+            if not self.orders[0]:
+                self.value = joined([part for part, _ in moved])
+                self.held = moved[0][1]
+                self.parts = None
+        elif self.last:
+            self.value = spread(self.value, self.last, self.held)
+            self.last = []
+
+    def values(self):
+        return [self.value] if self.parts is None else [part for part, _ in self.parts]
+
+    def put(self, values):
+        if self.parts is None:
+            self.value = values[0]
+        else:
+            self.parts = [(new, held) for new, (_, held) in zip(values, self.parts)]
+
+    def result(self):
+        return self.value.reshape((-1, self.width))
+
+
+def fold(value, hop, held):
+    axis, bit = hop
+    held = [item for item in held if item != hop]
+    dim = dim_of(axis, bit, held)
+    side = own_bit(axis, bit)
+    away = lax.dynamic_index_in_dim(value, 1 - side, dim, keepdims=False)
+    here = lax.dynamic_index_in_dim(value, side, dim, keepdims=False)
+    came = swap(away, axis, bit)
+    total = here.astype(jnp.float32) + came.astype(jnp.float32)
+    return total.astype(jnp.bfloat16), held
 
 
 class Reduction:
-    def __init__(self, grad, order):
+    def __init__(self, grad):
         dims, rows = place_dims(grad.shape[0])
         self.width = grad.shape[1]
         self.value = grad.astype(jnp.bfloat16).reshape(dims + (rows, self.width))
-        self.held = shard_route() + CORE + route(order)
-        self.down = CORE + route(order) + shard_route()[::-1]
-        self.up = route(1 - order) + CORE
+        self.held = shard_route() + CORE + route(0)
+        self.core, self.orders, self.near = CORE, [route(0), route(1)], shard_route()[::-1]
+        self.parts = None
+        self.back = None
 
     def live(self):
-        return bool(self.down or self.up)
+        return self.back is None or self.back.live()
 
     def step(self):
-        if self.down:
-            axis, bit = self.down.pop(0)
-            self.held.remove((axis, bit))
-            dim = dim_of(axis, bit, self.held)
-            side = own_bit(axis, bit)
-            away = lax.dynamic_index_in_dim(self.value, 1 - side, dim, keepdims=False)
-            here = lax.dynamic_index_in_dim(self.value, side, dim, keepdims=False)
-            came = swap(away, axis, bit)
-            total = here.astype(jnp.float32) + came.astype(jnp.float32)
-            self.value = total.astype(jnp.bfloat16)
-        elif self.up:
-            hop = self.up.pop(0)
-            self.value = spread(self.value, [hop], self.held)
-            self.held.append(hop)
+        if self.back is not None:
+            self.back.step()
+        elif self.core:
+            self.value, self.held = fold(self.value, self.core[0], self.held)
+            self.core = []
+        elif self.orders[0]:
+            if self.parts is None:
+                self.parts = [(part, self.held) for part in halved(self.value)]
+            self.parts = [
+                fold(part, order.pop(0), held)
+                for (part, held), order in zip(self.parts, self.orders)
+            ]
+            if not self.orders[0]:
+                self.value, self.held = joined([part for part, _ in self.parts]), self.parts[0][1]
+                self.parts = None
+        elif self.near:
+            self.value, self.held = fold(self.value, self.near.pop(0), self.held)
+            if not self.near:
+                self.back = Gather.__new__(Gather)
+                self.back.value, self.back.width, self.back.held = self.value, self.width, []
+                self.back.near, self.back.orders = [], [route(0), route(1)]
+                self.back.last, self.back.parts = CORE, None
+
+    def values(self):
+        if self.back is not None:
+            return self.back.values()
+        return [self.value] if self.parts is None else [part for part, _ in self.parts]
+
+    def put(self, values):
+        if self.back is not None:
+            self.back.put(values)
+        elif self.parts is None:
+            self.value = values[0]
+        else:
+            self.parts = [(new, held) for new, (_, held) in zip(values, self.parts)]
 
     def result(self):
-        return self.value.reshape((-1, self.width)).astype(jnp.float32)
-
-
-def tie(values, *reductions):
-    out = lax.optimization_barrier(tuple(values) + tuple(one.value for one in reductions))
-    for one, value in zip(reductions, out[len(values):]):
-        one.value = value
-    return out[: len(values)]
+        return self.back.result().astype(jnp.float32)
+
+
+def tie(values, *movers):
+    moving = [one.values() for one in movers]
+    out = lax.optimization_barrier((tuple(values), moving))
+    for one, new in zip(movers, out[1]):
+        one.put(new)
+    return out[0]
 
 
 def total_of(value):
@@ -169,11 +254,16 @@
     slim = spread(slim, shard_route(), [])
     slim = slim.reshape((-1,) + slim.shape[-2:]).swapaxes(0, 1).reshape(slim.shape[-2], -1)
     gain_first, gain_second, taps_full = slim[0], slim[1], slim[2:].T
-    in_full = gather_rows(in_weight, 1)
-    outw_full = gather_rows(out_weight, 0)
-    gate_full = gather_rows(gate_weight, 1)
-    up_full = gather_rows(up_weight, 0)
-    down_full = gather_rows(down_weight, 0)
+    gathers = [Gather(w) for w in (in_weight, out_weight, gate_weight, up_weight, down_weight)]
+    delays = [0, 0, 1, 2, 3]
+    turn = 0
+    while any(one.live() for one in gathers):
+        busy = [one for one, delay in zip(gathers, delays) if one.live() and turn >= delay]
+        for one in busy:
+            one.step()
+        tie((), *busy)
+        turn += 1
+    in_full, outw_full, gate_full, up_full, down_full = [one.result() for one in gathers]
     model_width = outw_full.shape[0]
     tok_count = tokens.shape[1]
     hidden = tokens[0].astype(jnp.float32)
@@ -210,7 +300,7 @@
     act_val = (silu_val * up_val).astype(jnp.bfloat16)
     cot_rows = cotangent[0]
     down_wgrad = over_rows(cot_rows, act_val)
-    down_red = Reduction(down_wgrad, 0)
+    down_red = Reduction(down_wgrad)
     (cot_back,) = tie((cot_rows,), down_red)
     act_back = plain_dot(cot_back, down_full)
     down_red.step()
@@ -220,10 +310,10 @@
     up_back = (act_back * silu_val).astype(jnp.bfloat16)
     gate_back, up_back = tie((gate_back, up_back), down_red)
     down_red.step()
-    gate_red = Reduction(over_rows(gate_back, normed_two), 1)
+    gate_red = Reduction(over_rows(gate_back, normed_two))
     (up_back,) = tie((up_back,), gate_red)
     gate_red.step()
-    up_red = Reduction(over_rows(up_back, normed_two), 0)
+    up_red = Reduction(over_rows(up_back, normed_two))
     up_back, gate_back = tie((up_back, gate_back), gate_red, up_red)
     gate_red.step()
     up_red.step()
@@ -236,7 +326,7 @@
     middle_back, gain_two_wgrad = norm_back(normed_two_back, middle, scale_two, gain_b)
     middle_back = middle_back + cot_rows.astype(jnp.float32)
     branch_back = middle_back.astype(jnp.bfloat16)
-    out_red = Reduction(over_rows(branch_back, mixed_in), 1)
+    out_red = Reduction(over_rows(branch_back, mixed_in))
     (branch_back,) = tie((branch_back,), out_red)
     out_red.step()
     mixin_back = plain_dot(branch_back, outw_full)
@@ -265,7 +355,7 @@
     out_red.step()
     down_red.step()
     gate_red.step()
-    in_red = Reduction(over_rows(proj_back, normed), 1)
+    in_red = Reduction(over_rows(proj_back, normed))
     proj_back, act_val = tie((proj_back, act_val), in_red)
     in_red.step()
     normed_back = plain_dot(proj_back, in_full)

time: 836 us -> 740 us (0.89)
  waiting for transfers between devices: 345 us -> 261 us
  starting transfers between devices: 169 us -> 144 us
  local copies, waits for them, and re-layouts: 41.7 us -> 55.6 us
    ppermute x72 -> x102, waiting for transfers between devices: 340 us -> 261 us  [swap(): lax.ppermute(value, axis, [(source, source ^ bit) for source in range(cou...]
    ppermute x2, starting transfers between devices: 25.7 us -> 3.95 us  [shifted(): lax.ppermute(value, axis, [(source, source + steps) for source in range(i...]
    select_n x40 -> x61, other arithmetic: 48 us -> 36.4 us  [spread(): jnp.where(mine, jnp.expand_dims(block, dim), jnp.expand_dims(other, dim))]
    ppermute x72 -> x102, starting transfers between devices: 143 us -> 140 us  [swap(): lax.ppermute(value, axis, [(source, source ^ bit) for source in range(cou...]
    squeeze x25 -> x35, local copies, waits for them, and re-layouts: 20.8 us -> 23.3 us  [fold(): away = lax.dynamic_index_in_dim(value, 1 - side, dim, keepdims=False)]
    convert_element_type x30 -> x40, other arithmetic: 54.9 us -> 55.3 us  [the longest x35 43.4 us: fold(): return (total.astype(jnp.bfloat16), held)]
  transfers between devices with their start and end apart: 74 -> 104, of which waited for: 31 -> 47; matrix products, arithmetic and copies ran while one was open for 30% -> 32% of each run, Pallas kernels for 0% -> 0%
where the time goes in v2:
time: 740 us; the launch traced here: 732 us
  waiting for transfers between devices  261 us (35%)
  starting transfers between devices  144 us (19%)
  matrix products  144 us (19%)
  other arithmetic  124 us (17%)
  local copies, waits for them, and re-layouts  55.6 us (8%)
    ppermute x102, waiting for transfers between devices, swap(): lax.ppermute(value, axis, [(source, source ^ bit) for source in range(cou...  261 us
    ppermute x102, starting transfers between devices, swap(): lax.ppermute(value, axis, [(source, source ^ bit) for source in range(cou...  140 us
    dot_general x5, matrix products, plain_dot(): return jnp.dot(left_side, weight, preferred_element_type=jnp.float32)  52.1 us
    dot_general x5, matrix products, times_rows(): lax.dot_general(left_side, weight, (((1,), (1,)), ((), ())), preferred_el...  51.4 us
    convert_element_type x35, other arithmetic, fold(): return (total.astype(jnp.bfloat16), held)  43.4 us
    dot_general x5, matrix products, over_rows(): lax.dot_general(left_side, right_side, (((0,), (0,)), ((), ())), preferre...  40.4 us
    select_n x61, other arithmetic, spread(): jnp.where(mine, jnp.expand_dims(block, dim), jnp.expand_dims(other, dim))  36.4 us
    squeeze x35, local copies, waits for them, and re-layouts, fold(): away = lax.dynamic_index_in_dim(value, 1 - side, dim, keepdims=False)  23.3 us
  transfers between devices with their start and end apart: 104, of which 47 were waited for; matrix products, arithmetic and copies ran while one was open for 32% of the time, Pallas kernels for 0%

profile of v2, /device:TPU:1, one launch (start us, length us, event | category | flops | bytes accessed | tf_op | source)
XLA Modules:
  0.0 731.9 jit_solution(2038228004484886153)
XLA Ops:
  15.9 7.1 collective-permute-done
  34.8 18.9 %collective-permute-done.4 = bf16[2,96,1024]{2,1,0:T(8,128)(2,1)S(1)} collective-permute-done((bf16[2,96,1024]{2,1,0:T(8,128)(2,1)S(1)}, bf16[2,96,1024]{2,1,0:T(8,128)(2,1)S(1)}, u32[]{:S(2)}, u32[]{:S(2)}) %collective-permute-start.4) | collective-permute-done | bytes 393248 | tf_op jit(solution)/shard_map/ppermute | solution.py:56
  59.4 4.0 collective-permute-done.8
  63.8 12.0 %collective-permute-done.11 = bf16[2,144,1024]{2,1,0:T(8,128)(2,1)S(1)} collective-permute-done((bf16[2,144,1024]{2,1,0:T(8,128)(2,1)S(1)}, bf16[2,144,1024]{2,1,0:T(8,128)(2,1)S(1)}, u32[]{:S(2)}, u32[]{:S(2)}) %collective-permute-start.11) | collective-permute-done | bytes 589856 | tf_op jit(solution)/shard_map/ppermute | solution.py:56
  84.2 8.1 %collective-permute-done.18 = bf16[2,2,72,1024]{3,2,1,0:T(8,128)(2,1)S(1)} collective-permute-done((bf16[2,2,72,1024]{3,2,1,0:T(8,128)(2,1)S(1)}, bf16[2,2,72,1024]{3,2,1,0:T(8,128)(2,1)S(1)}, u32[]{:S(2)}, u32[]{:S(2)}) %collective-permute-start.18) | collective-permute-done | bytes 589856 | tf_op jit(solution)/shard_map/ppermute | solution.py:56
  92.6 11.9 %collective-permute-done.19 = bf16[2,144,1024]{2,1,0:T(8,128)(2,1)S(1)} collective-permute-done((bf16[2,144,1024]{2,1,0:T(8,128)(2,1)S(1)}, bf16[2,144,1024]{2,1,0:T(8,128)(2,1)S(1)}, u32[]{:S(2)}, u32[]{:S(2)}) %collective-permute-start.19) | collective-permute-done | bytes 589856 | tf_op jit(solution)/shard_map/ppermute | solution.py:56
  104.7 4.5 collective-permute-done.13
  110.0 8.9 %collective-permute-start.21 = (bf16[2,2,2,2,96,1024]{5,4,3,2,1,0:T(8,128)(2,1)S(1)}, bf16[2,2,2,2,96,1024]{5,4,3,2,1,0:T(8,128)(2,1)}, u32[]{:S(2)}, u32[]{:S(2)}) collective-permute-start(bf16[2,2,2,2,96,1024]{5,4,3,2,1,0:T(8,128)(2,1)S(1)} %pad_maximum_fusion.4), channel_id=1, source_target_pairs={{0,1},{1,0},{2,3},{3,2},{4,5},{5,4},{6,7},{7,6},{8,9},{9,8},{10,11... | collective-permute-start | bytes 9437192 | tf_op jit(solution)/shard_map/ppermute | solution.py:56
  121.0 18.5 %collective-permute-start.22 = (bf16[2,2,2,2,32,1024]{5,4,3,2,1,0:T(8,128)(2,1)S(1)}, bf16[2,2,2,2,32,1024]{5,4,3,2,1,0:T(8,128)(2,1)S(1)}, u32[]{:S(2)}, u32[]{:S(2)}) collective-permute-start(bf16[2,2,2,2,32,1024]{5,4,3,2,1,0:T(8,128)(2,1)S(1)} %pad_maximum_fusion.11), channel_id=1, source_target_pairs={{0,1},{1,0},{2,3},{3,2},{4,5},{5,4},{6,7},{7,6},{8,9},{9,8},{10,11... | collective-permute-start | bytes 3145736 | tf_op jit(solution)/shard_map/ppermute | solution.py:56
  146.0 13.3 %collective-permute-done.23 = bf16[2,2,2,72,1024]{4,3,2,1,0:T(8,128)(2,1)S(1)} collective-permute-done((bf16[2,2,2,72,1024]{4,3,2,1,0:T(8,128)(2,1)S(1)}, bf16[2,2,2,72,1024]{4,3,2,1,0:T(8,128)(2,1)S(1)}, u32[]{:S(2)}, u32[]{:S(2)}) %collective-permute-start.23) | collective-permute-done | bytes 1179680 | tf_op jit(solution)/shard_map/ppermute | solution.py:56
  159.5 8.8 %collective-permute-done.24 = bf16[2,2,2,72,1024]{4,3,2,1,0:T(8,128)(2,1)S(1)} collective-permute-done((bf16[2,2,2,72,1024]{4,3,2,1,0:T(8,128)(2,1)S(1)}, bf16[2,2,2,72,1024]{4,3,2,1,0:T(8,128)(2,1)S(1)}, u32[]{:S(2)}, u32[]{:S(2)}) %collective-permute-start.24) | collective-permute-done | bytes 1179680 | tf_op jit(solution)/shard_map/ppermute | solution.py:56
  171.4 5.1 broadcast_select_fusion.3
  176.5 7.5 %fusion.35 = f32[768,3072]{1,0:T(8,128)S(1)} fusion(bf16[3072,1024]{1,0:T(8,128)(2,1)} %bitcast.329, bf16[1,768,1024]{2,1,0:T(8,128)(2,1)S(1)} %copy-done.15, f32[1024]{0:T(1024)S(1)} %bitcast.357, f32[768]{0:T(1024)S(1)} %get-tuple-element.253), kind=kOutput, calls=%fused_computation.105 | convolution fusion | flops 4834983936 | bytes 17308672 | tf_op jit(solution)/shard_map/dot_general | solution.py:16
  202.0 24.5 %collective-permute-done.30 = bf16[2,2,2,72,1024]{4,3,2,1,0:T(8,128)(2,1)S(1)} collective-permute-done((bf16[2,2,2,72,1024]{4,3,2,1,0:T(8,128)(2,1)S(1)}, bf16[2,2,2,72,1024]{4,3,2,1,0:T(8,128)(2,1)S(1)}, u32[]{:S(2)}, u32[]{:S(2)}) %collective-permute-start.30) | collective-permute-done | bytes 1179680 | tf_op jit(solution)/shard_map/ppermute | solution.py:56
  227.6 6.6 broadcast_select_fusion.2
  239.0 13.7 %fusion.86 = f32[768,4608]{1,0:T(8,128)} fusion(bf16[768,1024]{1,0:T(8,128)(2,1)S(1)} %multiply_convert_fusion.7, bf16[4608,1024]{1,0:T(8,128)(2,1)} %bitcast.313), kind=kOutput, calls=%fused_computation.302 | convolution fusion | flops 7247757312 | bytes 25165824 | tf_op jit(solution)/shard_map/dot_general | solution.py:16
  252.7 6.7 collective-permute-done.35
  262.8 4.1 broadcast_select_fusion.1
  270.4 17.4 %multiply_convert_fusion.2 = (bf16[768,4608]{1,0:T(8,128)(2,1)}, f32[768,4608]{1,0:T(8,128)}) fusion(f32[768,4608]{1,0:T(8,128)} %fusion.86, bf16[768,1024]{1,0:T(8,128)(2,1)} %copy-done.35, bf16[4608,1024]{1,0:T(8,128)(2,1)} %bitcast.317), kind=kOutput, calls=%fused_computation.2 | convolution fusion | flops 7268990976 | bytes 46399488 | tf_op jit(solution)/shard_map/dot_general | solution.py:16
  287.8 11.0 %convolution_convert_fusion.2 = bf16[4608,1024]{0,1:T(8,128)(2,1)S(1)} fusion(bf16[768,4608]{1,0:T(8,128)(2,1)} %get-tuple-element.163, bf16[1,768,1024]{2,1,0:T(8,128)(2,1)S(1)} %copy-done.33), kind=kOutput, calls=%fused_computation.7 | convolution fusion | flops 7252475904 | bytes 18087936 | tf_op jit(solution)/shard_map/dot_general | solution.py:22
  303.8 7.7 %broadcast_select_fusion = bf16[2,2,2,2,2,32,4608]{6,5,4,3,2,1,0:T(8,128)(2,1)} fusion(pred[2]{0:T(512)(128)(4,1)S(1)} %iota_compare_fusion.3, bf16[2,2,2,2,32,4608]{5,4,3,2,1,0:T(8,128)(2,1)} %collective-permute-done.37, bf16[2,2,2,2,32,4608]{5,4,3,2,1,0:T(8,128)(2,1)} %pad_maximum_fusion.2), kind=kLoop, calls=%fused_computation.14 | loop fusion | flops 4718592 | bytes 18874370 | tf_op jit(solution)/shard_map/jit(_where)/select_n | solution.py:96
  311.5 22.5 %multiply_convert_fusion = (bf16[768,4608]{1,0:T(8,128)(2,1)}, bf16[768,4608]{1,0:T(8,128)(2,1)}) fusion(f32[768,4608]{1,0:T(8,128)} %fusion.86, f32[768,4608]{1,0:T(8,128)} %get-tuple-element.267, bf16[768,1024]{1,0:T(8,128)(2,1)S(1)} %bitcast.339, bf16[1024,4608]{1,0:T(8,128)(2,1)} %bitcast.309), kind=kOutput, calls=%fused_computation | convolution fusion | flops 7293763584 | bytes 53477376 | tf_op jit(solution)/shard_map/dot_general | solution.py:28
  334.0 7.5 %fusion.3 = bf16[2,2,2,2,32,4608]{5,4,3,2,1,0:T(8,128)(2,1)} fusion(bf16[2,2,2,2,32,4608]{5,4,3,2,1,0:T(8,128)(2,1)} %collective-permute-done.38, bf16[2,2,2,2,2,32,4608]{6,5,4,3,2,1,0:T(8,128)(2,1)} %bitcast.328, s32[]{:T(128)S(6)} %select_n.734), kind=kLoop, calls=%fused_computation.13 | loop fusion | flops 9437184 | bytes 14155780 | tf_op jit(solution)/shard_map/convert_element_type | solution.py:168
  341.5 8.2 %convolution_convert_fusion.1 = bf16[4608,1024]{1,0:T(8,128)(2,1)S(1)} fusion(bf16[768,4608]{1,0:T(8,128)(2,1)S(1)} %copy-done.73, bf16[768,1024]{1,0:T(8,128)(2,1)S(1)} %copy-done.36), kind=kOutput, calls=%fused_computation.6 | convolution fusion | flops 7252475904 | bytes 18087936 | tf_op jit(solution)/shard_map/dot_general | solution.py:22
  361.2 13.5 %convolution_convert_fusion = bf16[4608,1024]{1,0:T(8,128)(2,1)} fusion(bf16[768,4608]{1,0:T(8,128)(2,1)} %get-tuple-element.146, bf16[768,1024]{1,0:T(8,128)(2,1)S(1)} %copy-done.37), kind=kOutput, calls=%fused_computation.5 | convolution fusion | flops 7252475904 | bytes 18087936 | tf_op jit(solution)/shard_map/dot_general | solution.py:22
  376.7 4.7 fusion.2
  390.2 13.6 %collective-permute-done.41 = bf16[2,2,2,16,4608]{4,3,1,0,2:T(8,128)(2,1)} collective-permute-done((bf16[2,2,2,16,4608]{4,3,1,0,2:T(8,128)(2,1)}, bf16[2,2,2,16,4608]{4,3,1,0,2:T(8,128)(2,1)}, u32[]{:S(2)}, u32[]{:S(2)}) %collective-permute-start.41) | collective-permute-done | bytes 1179680 | tf_op jit(solution)/shard_map/ppermute | solution.py:56
  410.4 11.5 %fusion.87 = f32[768,1024]{1,0:T(8,128)} fusion(bf16[768,4608]{1,0:T(8,128)(2,1)} %get-tuple-element.142, bf16[4608,1024]{1,0:T(8,128)(2,1)S(1)} %bitcast.316), kind=kOutput, calls=%fused_computation.303 | convolution fusion | flops 7247757312 | bytes 19660800 | tf_op jit(solution)/shard_map/dot_general | solution.py:28
  421.9 12.6 %collective-permute-done.48 = bf16[2,2,2,72,1024]{4,3,2,1,0:T(8,128)(2,1)S(1)} collective-permute-done((bf16[2,2,2,72,1024]{4,3,2,1,0:T(8,128)(2,1)S(1)}, bf16[2,2,2,72,1024]{4,3,2,1,0:T(8,128)(2,1)S(1)}, u32[]{:S(2)}, u32[]{:S(2)}) %collective-permute-start.48) | collective-permute-done | bytes 1179680 | tf_op jit(solution)/shard_map/ppermute | solution.py:56
  437.6 6.4 fusion.1
  449.2 7.5 %fusion.88 = f32[768,1024]{1,0:T(8,128)S(1)} fusion(bf16[768,4608]{1,0:T(8,128)(2,1)S(1)} %bitcast.368, bf16[4608,1024]{1,0:T(8,128)(2,1)S(1)} %bitcast.320), kind=kOutput, calls=%fused_computation.304 | convolution fusion | flops 7247757312 | bytes 19660800 | tf_op jit(solution)/shard_map/dot_general | solution.py:28
  473.5 4.4 multiply_convert_fusion.4
  484.7 4.0 multiply_reduce_fusion.2
  496.6 5.9 convolution_convert_fusion.3
  506.3 7.1 fusion.20
  515.6 4.5 fusion.17
  543.8 6.0 collective-permute-done.51
  550.2 15.0 %collective-permute-done.49 = bf16[2,32,4608]{2,1,0:T(8,128)(2,1)S(1)} collective-permute-done((bf16[2,32,4608]{2,1,0:T(8,128)(2,1)S(1)}, bf16[2,32,4608]{2,1,0:T(8,128)(2,1)S(1)}, u32[]{:S(2)}, u32[]{:S(2)}) %collective-permute-start.49) | collective-permute-done | bytes 589856 | tf_op jit(solution)/shard_map/ppermute | solution.py:56
  576.5 10.9 %fusion.44 = bf16[1,768,1024]{2,1,0:T(8,128)(2,1)} fusion(f32[768,1024]{1,0:T(8,128)S(1)} %copy-done.7, bf16[768,4608]{1,0:T(8,128)(2,1)} %get-tuple-element.163, bf16[1024,4608]{1,0:T(8,128)(2,1)S(1)} %bitcast.312), kind=kOutput, calls=%fused_computation.118 | convolution fusion | flops 7249330176 | bytes 21233664 | tf_op jit(solution)/shard_map/dot_general | solution.py:16
  595.1 4.4 collective-permute-done.62
  605.1 23.7 %collective-permute-done.63 = bf16[2,144,1024]{2,1,0:T(8,128)(2,1)S(1)} collective-permute-done((bf16[2,144,1024]{2,1,0:T(8,128)(2,1)S(1)}, bf16[2,144,1024]{2,1,0:T(8,128)(2,1)S(1)}, u32[]{:S(2)}, u32[]{:S(2)}) %collective-permute-start.63) | collective-permute-done | bytes 589856 | tf_op jit(solution)/shard_map/ppermute | solution.py:56
  637.9 4.6 collective-permute-done.71
  646.6 7.2 collective-permute-done.72
  654.2 10.5 %collective-permute-done.73 = bf16[2,144,1024]{2,1,0:T(8,128)(2,1)S(1)} collective-permute-done((bf16[2,144,1024]{2,1,0:T(8,128)(2,1)S(1)}, bf16[2,144,1024]{2,1,0:T(8,128)(2,1)S(1)}, u32[]{:S(2)}, u32[]{:S(2)}) %collective-permute-start.73) | collective-permute-done | bytes 589856 | tf_op jit(solution)/shard_map/ppermute | solution.py:56
  665.2 3.9 collective-permute-start.82
  674.3 4.1 collective-permute-done.77
  679.7 4.4 collective-permute-done.83
  689.4 7.1 collective-permute-start.84
  (608 shorter events, 272.5 us)
Async XLA Ops:
  1.7 26.4 %collective-permute-start.3 = (bf16[32,1024]{1,0:T(8,128)(2,1)S(1)}, bf16[32,1024]{1,0:T(8,128)(2,1)S(1)}, u32[]{:S(2)}, u32[]{:S(2)}) collective-permute-start(bf16[32,1024]{1,0:T(8,128)(2,1)S(1)} %constant_dynamic-slice_fusion.5), channel_id=1, source_target_pairs={{0,8},{8,0},{16,24},{24,16},{1,9},{9,1},{17,25},{25,17},{2,10},{10... | collective-permute-start | bytes 196616 | tf_op jit(solution)/shard_map/ppermute | solution.py:56
  4.7 23.4 %collective-permute-start.2 = (bf16[96,1024]{1,0:T(8,128)(2,1)S(1)}, bf16[96,1024]{1,0:T(8,128)(2,1)S(1)}, u32[]{:S(2)}, u32[]{:S(2)}) collective-permute-start(bf16[96,1024]{1,0:T(8,128)(2,1)S(1)} %constant_dynamic-slice_fusion.6), channel_id=1, source_target_pairs={{0,8},{8,0},{16,24},{24,16},{1,9},{9,1},{17,25},{25,17},{2,10},{10... | collective-permute-start | bytes 589832 | tf_op jit(solution)/shard_map/ppermute | solution.py:56
  4.9 29.3 %collective-permute-start.12 = (bf16[144,1024]{1,0:T(8,128)(2,1)S(1)}, bf16[144,1024]{1,0:T(8,128)(2,1)S(1)}, u32[]{:S(2)}, u32[]{:S(2)}) collective-permute-start(bf16[144,1024]{1,0:T(8,128)(2,1)S(1)} %constant_dynamic-slice_fusion.3), channel_id=1, source_target_pairs={{0,8},{8,0},{16,24},{24,16},{1,9},{9,1},{17,25},{25,17},{2,10},{10... | collective-permute-start | bytes 884744 | tf_op jit(solution)/shard_map/ppermute | solution.py:56
  7.4 26.8 %collective-permute-start.6 = (bf16[144,1024]{1,0:T(8,128)(2,1)S(1)}, bf16[144,1024]{1,0:T(8,128)(2,1)S(1)}, u32[]{:S(2)}, u32[]{:S(2)}) collective-permute-start(bf16[144,1024]{1,0:T(8,128)(2,1)S(1)} %constant_dynamic-slice_fusion.4), channel_id=1, source_target_pairs={{0,8},{8,0},{16,24},{24,16},{1,9},{9,1},{17,25},{25,17},{2,10},{10... | collective-permute-start | bytes 884744 | tf_op jit(solution)/shard_map/ppermute | solution.py:56
  30.7 23.1 %collective-permute-start.4 = (bf16[2,96,1024]{2,1,0:T(8,128)(2,1)S(1)}, bf16[2,96,1024]{2,1,0:T(8,128)(2,1)S(1)}, u32[]{:S(2)}, u32[]{:S(2)}) collective-permute-start(bf16[2,96,1024]{2,1,0:T(8,128)(2,1)S(1)} %broadcast_select_fusion.43), channel_id=1, source_target_pairs={{0,16},{8,24},{16,0},{24,8},{1,17},{9,25},{17,1},{25,9},{2,18},{10... | collective-permute-start | bytes 1179656 | tf_op jit(solution)/shard_map/ppermute | solution.py:56
  53.9 22.0 %collective-permute-start.11 = (bf16[2,144,1024]{2,1,0:T(8,128)(2,1)S(1)}, bf16[2,144,1024]{2,1,0:T(8,128)(2,1)S(1)}, u32[]{:S(2)}, u32[]{:S(2)}) collective-permute-start(bf16[2,144,1024]{2,1,0:T(8,128)(2,1)S(1)} %get-tuple-element.111), channel_id=1, source_target_pairs={{0,16},{8,24},{16,0},{24,8},{1,17},{9,25},{17,1},{25,9},{2,18},{10... | collective-permute-start | bytes 1769480 | tf_op jit(solution)/shard_map/ppermute | solution.py:56
  79.2 25.3 %collective-permute-start.19 = (bf16[2,144,1024]{2,1,0:T(8,128)(2,1)S(1)}, bf16[2,144,1024]{2,1,0:T(8,128)(2,1)S(1)}, u32[]{:S(2)}, u32[]{:S(2)}) collective-permute-start(bf16[2,144,1024]{2,1,0:T(8,128)(2,1)S(1)} %get-tuple-element.117), channel_id=1, source_target_pairs={{0,16},{8,24},{16,0},{24,8},{1,17},{9,25},{17,1},{25,9},{2,18},{10... | collective-permute-start | bytes 1769480 | tf_op jit(solution)/shard_map/ppermute | solution.py:56
  81.8 27.3 %collective-permute-start.13 = (bf16[2,2,2,48,1024]{4,3,2,1,0:T(8,128)(2,1)S(1)}, bf16[2,2,2,48,1024]{4,3,2,1,0:T(8,128)(2,1)S(1)}, u32[]{:S(2)}, u32[]{:S(2)}) collective-permute-start(bf16[2,2,2,48,1024]{4,3,2,1,0:T(8,128)(2,1)S(1)} %broadcast_select_fusion.28), channel_id=1, source_target_pairs={{0,4},{1,5},{2,6},{3,7},{4,0},{5,1},{6,2},{7,3},{8,12},{9,13},{10,... | collective-permute-start | bytes 2359304 | tf_op jit(solution)/shard_map/ppermute | solution.py:56
  82.7 26.6 %collective-permute-start.14 = (bf16[2,2,2,48,1024]{4,3,2,1,0:T(8,128)(2,1)S(1)}, bf16[2,2,2,48,1024]{4,3,2,1,0:T(8,128)(2,1)S(1)}, u32[]{:S(2)}, u32[]{:S(2)}) collective-permute-start(bf16[2,2,2,48,1024]{4,3,2,1,0:T(8,128)(2,1)S(1)} %broadcast_select_fusion.26), channel_id=1, source_target_pairs={{0,2},{1,3},{2,0},{3,1},{4,6},{5,7},{6,4},{7,5},{8,10},{9,11},{10,... | collective-permute-start | bytes 2359304 | tf_op jit(solution)/shard_map/ppermute | solution.py:56
  110.0 61.4 %collective-permute-start.21 = (bf16[2,2,2,2,96,1024]{5,4,3,2,1,0:T(8,128)(2,1)S(1)}, bf16[2,2,2,2,96,1024]{5,4,3,2,1,0:T(8,128)(2,1)}, u32[]{:S(2)}, u32[]{:S(2)}) collective-permute-start(bf16[2,2,2,2,96,1024]{5,4,3,2,1,0:T(8,128)(2,1)S(1)} %pad_maximum_fusion.4), channel_id=1, source_target_pairs={{0,1},{1,0},{2,3},{3,2},{4,5},{5,4},{6,7},{7,6},{8,9},{9,8},{10,11... | collective-permute-start | bytes 9437192 | tf_op jit(solution)/shard_map/ppermute | solution.py:56
  119.0 21.8 %collective-permute-start.26 = (bf16[2,2,72,1024]{3,2,1,0:T(8,128)(2,1)S(1)}, bf16[2,2,72,1024]{3,2,1,0:T(8,128)(2,1)S(1)}, u32[]{:S(2)}, u32[]{:S(2)}) collective-permute-start(bf16[2,2,72,1024]{3,2,1,0:T(8,128)(2,1)S(1)} %get-tuple-element.227), channel_id=1, source_target_pairs={{0,4},{1,5},{2,6},{3,7},{4,0},{5,1},{6,2},{7,3},{8,12},{9,13},{10,... | collective-permute-start | bytes 1769480 | tf_op jit(solution)/shard_map/ppermute | solution.py:56
  120.3 22.9 %collective-permute-start.25 = (bf16[2,2,72,1024]{3,2,1,0:T(8,128)(2,1)S(1)}, bf16[2,2,72,1024]{3,2,1,0:T(8,128)(2,1)S(1)}, u32[]{:S(2)}, u32[]{:S(2)}) collective-permute-start(bf16[2,2,72,1024]{3,2,1,0:T(8,128)(2,1)S(1)} %get-tuple-element.228), channel_id=1, source_target_pairs={{0,2},{1,3},{2,0},{3,1},{4,6},{5,7},{6,4},{7,5},{8,10},{9,11},{10,... | collective-permute-start | bytes 1769480 | tf_op jit(solution)/shard_map/ppermute | solution.py:56
  120.6 38.7 %collective-permute-start.23 = (bf16[2,2,2,72,1024]{4,3,2,1,0:T(8,128)(2,1)S(1)}, bf16[2,2,2,72,1024]{4,3,2,1,0:T(8,128)(2,1)S(1)}, u32[]{:S(2)}, u32[]{:S(2)}) collective-permute-start(bf16[2,2,2,72,1024]{4,3,2,1,0:T(8,128)(2,1)S(1)} %broadcast_select_fusion.23), channel_id=1, source_target_pairs={{0,4},{1,5},{2,6},{3,7},{4,0},{5,1},{6,2},{7,3},{8,12},{9,13},{10,... | collective-permute-start | bytes 3538952 | tf_op jit(solution)/shard_map/ppermute | solution.py:56
  121.0 23.3 %collective-permute-start.22 = (bf16[2,2,2,2,32,1024]{5,4,3,2,1,0:T(8,128)(2,1)S(1)}, bf16[2,2,2,2,32,1024]{5,4,3,2,1,0:T(8,128)(2,1)S(1)}, u32[]{:S(2)}, u32[]{:S(2)}) collective-permute-start(bf16[2,2,2,2,32,1024]{5,4,3,2,1,0:T(8,128)(2,1)S(1)} %pad_maximum_fusion.11), channel_id=1, source_target_pairs={{0,1},{1,0},{2,3},{3,2},{4,5},{5,4},{6,7},{7,6},{8,9},{9,8},{10,11... | collective-permute-start | bytes 3145736 | tf_op jit(solution)/shard_map/ppermute | solution.py:56
  140.8 27.6 %collective-permute-start.24 = (bf16[2,2,2,72,1024]{4,3,2,1,0:T(8,128)(2,1)S(1)}, bf16[2,2,2,72,1024]{4,3,2,1,0:T(8,128)(2,1)S(1)}, u32[]{:S(2)}, u32[]{:S(2)}) collective-permute-start(bf16[2,2,2,72,1024]{4,3,2,1,0:T(8,128)(2,1)S(1)} %broadcast_select_fusion.21), channel_id=1, source_target_pairs={{0,2},{1,3},{2,0},{3,1},{4,6},{5,7},{6,4},{7,5},{8,10},{9,11},{10,... | collective-permute-start | bytes 3538952 | tf_op jit(solution)/shard_map/ppermute | solution.py:56
  189.2 37.3 %collective-permute-start.30 = (bf16[2,2,2,72,1024]{4,3,2,1,0:T(8,128)(2,1)S(1)}, bf16[2,2,2,72,1024]{4,3,2,1,0:T(8,128)(2,1)S(1)}, u32[]{:S(2)}, u32[]{:S(2)}) collective-permute-start(bf16[2,2,2,72,1024]{4,3,2,1,0:T(8,128)(2,1)S(1)} %copy-done.19), channel_id=1, source_target_pairs={{0,4},{1,5},{2,6},{3,7},{4,0},{5,1},{6,2},{7,3},{8,12},{9,13},{10,... | collective-permute-start | bytes 3538952 | tf_op jit(solution)/shard_map/ppermute | solution.py:56
  190.0 36.8 %collective-permute-start.31 = (bf16[2,2,2,72,1024]{4,3,2,1,0:T(8,128)(2,1)S(1)}, bf16[2,2,2,72,1024]{4,3,2,1,0:T(8,128)(2,1)S(1)}, u32[]{:S(2)}, u32[]{:S(2)}) collective-permute-start(bf16[2,2,2,72,1024]{4,3,2,1,0:T(8,128)(2,1)S(1)} %copy-done.18), channel_id=1, source_target_pairs={{0,2},{1,3},{2,0},{3,1},{4,6},{5,7},{6,4},{7,5},{8,10},{9,11},{10,... | collective-permute-start | bytes 3538952 | tf_op jit(solution)/shard_map/ppermute | solution.py:56
  190.4 37.2 %collective-permute-start.29 = (bf16[2,2,2,2,144,1024]{5,4,3,2,1,0:T(8,128)(2,1)S(1)}, bf16[2,2,2,2,144,1024]{5,4,3,2,1,0:T(8,128)(2,1)}, u32[]{:S(2)}, u32[]{:S(2)}) collective-permute-start(bf16[2,2,2,2,144,1024]{5,4,3,2,1,0:T(8,128)(2,1)S(1)} %bitcast.306), channel_id=1, source_target_pairs={{0,1},{1,0},{2,3},{3,2},{4,5},{5,4},{6,7},{7,6},{8,9},{9,8},{10,11... | collective-permute-start | bytes 14155784 | tf_op jit(solution)/shard_map/ppermute | solution.py:56
  234.2 25.2 %collective-permute-start.35 = (bf16[2,2,2,16,4608]{4,3,2,1,0:T(8,128)(2,1)S(1)}, bf16[2,2,2,16,4608]{4,3,2,1,0:T(8,128)(2,1)S(1)}, u32[]{:S(2)}, u32[]{:S(2)}) collective-permute-start(bf16[2,2,2,16,4608]{4,3,2,1,0:T(8,128)(2,1)S(1)} %broadcast_select_fusion.18), channel_id=1, source_target_pairs={{0,4},{1,5},{2,6},{3,7},{4,0},{5,1},{6,2},{7,3},{8,12},{9,13},{10,... | collective-permute-start | bytes 3538952 | tf_op jit(solution)/shard_map/ppermute | solution.py:56
  235.2 24.9 %collective-permute-start.36 = (bf16[2,2,2,16,4608]{4,3,2,1,0:T(8,128)(2,1)S(1)}, bf16[2,2,2,16,4608]{4,3,2,1,0:T(8,128)(2,1)S(1)}, u32[]{:S(2)}, u32[]{:S(2)}) collective-permute-start(bf16[2,2,2,16,4608]{4,3,2,1,0:T(8,128)(2,1)S(1)} %broadcast_select_fusion.17), channel_id=1, source_target_pairs={{0,2},{1,3},{2,0},{3,1},{4,6},{5,7},{6,4},{7,5},{8,10},{9,11},{10,... | collective-permute-start | bytes 3538952 | tf_op jit(solution)/shard_map/ppermute | solution.py:56
  236.2 26.6 %collective-permute-start.34 = (bf16[2,2,2,2,144,1024]{5,4,3,2,1,0:T(8,128)(2,1)S(1)}, bf16[2,2,2,2,144,1024]{5,4,3,2,1,0:T(8,128)(2,1)S(1)}, u32[]{:S(2)}, u32[]{:S(2)}) collective-permute-start(bf16[2,2,2,2,144,1024]{5,4,3,2,1,0:T(8,128)(2,1)S(1)} %pad_maximum_fusion.1), channel_id=1, source_target_pairs={{0,1},{1,0},{2,3},{3,2},{4,5},{5,4},{6,7},{7,6},{8,9},{9,8},{10,11... | collective-permute-start | bytes 14155784 | tf_op jit(solution)/shard_map/ppermute | solution.py:56
  266.9 36.9 %collective-permute-start.37 = (bf16[2,2,2,2,32,4608]{5,4,3,2,1,0:T(8,128)(2,1)}, bf16[2,2,2,2,32,4608]{5,4,3,2,1,0:T(8,128)(2,1)}, u32[]{:S(2)}, u32[]{:S(2)}) collective-permute-start(bf16[2,2,2,2,32,4608]{5,4,3,2,1,0:T(8,128)(2,1)} %pad_maximum_fusion.2), channel_id=1, source_target_pairs={{0,1},{1,0},{2,3},{3,2},{4,5},{5,4},{6,7},{7,6},{8,9},{9,8},{10,11... | collective-permute-start | bytes 14155784 | tf_op jit(solution)/shard_map/ppermute | solution.py:56
  303.8 30.2 %collective-permute-start.38 = (bf16[2,2,2,2,32,4608]{5,4,3,2,1,0:T(8,128)(2,1)}, bf16[2,2,2,2,32,4608]{5,4,3,2,1,0:T(8,128)(2,1)}, u32[]{:S(2)}, u32[]{:S(2)}) collective-permute-start(bf16[2,2,2,2,32,4608]{5,4,3,2,1,0:T(8,128)(2,1)} %dynamic-slice_bitcast_fusion.2), channel_id=1, source_target_pairs={{0,1},{1,0},{2,3},{3,2},{4,5},{5,4},{6,7},{7,6},{8,9},{9,8},{10,11... | collective-permute-start | bytes 14155784 | tf_op jit(solution)/shard_map/ppermute | solution.py:56
  354.7 22.0 %collective-permute-start.39 = (bf16[2,2,2,2,144,1024]{5,4,3,2,1,0:T(8,128)(2,1)}, bf16[2,2,2,2,144,1024]{5,4,3,2,1,0:T(8,128)(2,1)}, u32[]{:S(2)}, u32[]{:S(2)}) collective-permute-start(bf16[2,2,2,2,144,1024]{5,4,3,2,1,0:T(8,128)(2,1)} %dynamic-slice_bitcast_fusion.1), channel_id=1, source_target_pairs={{0,1},{1,0},{2,3},{3,2},{4,5},{5,4},{6,7},{7,6},{8,9},{9,8},{10,11... | collective-permute-start | bytes 14155784 | tf_op jit(solution)/shard_map/ppermute | solution.py:56
  359.8 27.9 %collective-permute-start.42 = (bf16[2,2,2,16,4608]{4,3,2,1,0:T(8,128)(2,1)}, bf16[2,2,2,16,4608]{4,3,2,1,0:T(8,128)(2,1)}, u32[]{:S(2)}, u32[]{:S(2)}) collective-permute-start(bf16[2,2,2,16,4608]{4,3,2,1,0:T(8,128)(2,1)} %dynamic-slice_bitcast_fusion.8), channel_id=1, source_target_pairs={{0,4},{1,5},{2,6},{3,7},{4,0},{5,1},{6,2},{7,3},{8,12},{9,13},{10,... | collective-permute-start | bytes 3538952 | tf_op jit(solution)/shard_map/ppermute | solution.py:56
  375.8 28.0 %collective-permute-start.41 = (bf16[2,2,2,16,4608]{4,3,1,0,2:T(8,128)(2,1)}, bf16[2,2,2,16,4608]{4,3,1,0,2:T(8,128)(2,1)}, u32[]{:S(2)}, u32[]{:S(2)}) collective-permute-start(bf16[2,2,2,16,4608]{4,3,1,0,2:T(8,128)(2,1)} %dynamic-slice_bitcast_fusion.9), channel_id=1, source_target_pairs={{0,2},{1,3},{2,0},{3,1},{4,6},{5,7},{6,4},{7,5},{8,10},{9,11},{10,... | collective-permute-start | bytes 3538952 | tf_op jit(solution)/shard_map/ppermute | solution.py:56
  384.3 53.2 %collective-permute-start.40 = (bf16[2,2,2,2,144,1024]{5,4,3,2,1,0:T(8,128)(2,1)S(1)}, bf16[2,2,2,2,144,1024]{5,4,3,2,1,0:T(8,128)(2,1)}, u32[]{:S(2)}, u32[]{:S(2)}) collective-permute-start(bf16[2,2,2,2,144,1024]{5,4,3,2,1,0:T(8,128)(2,1)S(1)} %dynamic-slice_bitcast_fusion), channel_id=1, source_target_pairs={{0,1},{1,0},{2,3},{3,2},{4,5},{5,4},{6,7},{7,6},{8,9},{9,8},{10,11... | collective-permute-start | bytes 14155784 | tf_op jit(solution)/shard_map/ppermute | solution.py:56
  407.6 26.9 %collective-permute-start.48 = (bf16[2,2,2,72,1024]{4,3,2,1,0:T(8,128)(2,1)S(1)}, bf16[2,2,2,72,1024]{4,3,2,1,0:T(8,128)(2,1)S(1)}, u32[]{:S(2)}, u32[]{:S(2)}) collective-permute-start(bf16[2,2,2,72,1024]{4,3,2,1,0:T(8,128)(2,1)S(1)} %dynamic-slice_bitcast_fusion.6), channel_id=1, source_target_pairs={{0,4},{1,5},{2,6},{3,7},{4,0},{5,1},{6,2},{7,3},{8,12},{9,13},{10,... | collective-permute-start | bytes 3538952 | tf_op jit(solution)/shard_map/ppermute | solution.py:56
  408.3 27.7 %collective-permute-start.47 = (bf16[2,2,2,72,1024]{4,3,1,0,2:T(8,128)(2,1)S(1)}, bf16[2,2,2,72,1024]{4,3,1,0,2:T(8,128)(2,1)S(1)}, u32[]{:S(2)}, u32[]{:S(2)}) collective-permute-start(bf16[2,2,2,72,1024]{4,3,1,0,2:T(8,128)(2,1)S(1)} %dynamic-slice_bitcast_fusion.7), channel_id=1, source_target_pairs={{0,2},{1,3},{2,0},{3,1},{4,6},{5,7},{6,4},{7,5},{8,10},{9,11},{10,... | collective-permute-start | bytes 3538952 | tf_op jit(solution)/shard_map/ppermute | solution.py:56
  458.8 32.1 %collective-permute-start.45 = (bf16[2,2,16,4608]{3,2,1,0:T(8,128)(2,1)}, bf16[2,2,16,4608]{3,2,1,0:T(8,128)(2,1)}, u32[]{:S(2)}, u32[]{:S(2)}) collective-permute-start(bf16[2,2,16,4608]{3,2,1,0:T(8,128)(2,1)} %dynamic-slice_bitcast_fusion.21), channel_id=1, source_target_pairs={{0,4},{1,5},{2,6},{3,7},{4,0},{5,1},{6,2},{7,3},{8,12},{9,13},{10,... | collective-permute-start | bytes 1769480 | tf_op jit(solution)/shard_map/ppermute | solution.py:56
  459.9 33.1 %collective-permute-start.46 = (bf16[2,2,16,4608]{3,2,1,0:T(8,128)(2,1)}, bf16[2,2,16,4608]{3,2,1,0:T(8,128)(2,1)}, u32[]{:S(2)}, u32[]{:S(2)}) collective-permute-start(bf16[2,2,16,4608]{3,2,1,0:T(8,128)(2,1)} %dynamic-slice_bitcast_fusion.20), channel_id=1, source_target_pairs={{0,2},{1,3},{2,0},{3,1},{4,6},{5,7},{6,4},{7,5},{8,10},{9,11},{10,... | collective-permute-start | bytes 1769480 | tf_op jit(solution)/shard_map/ppermute | solution.py:56
  467.8 26.7 %collective-permute-start.44 = (bf16[2,2,2,2,32,1024]{5,4,3,2,1,0:T(8,128)(2,1)}, bf16[2,2,2,2,32,1024]{5,4,3,2,1,0:T(8,128)(2,1)}, u32[]{:S(2)}, u32[]{:S(2)}) collective-permute-start(bf16[2,2,2,2,32,1024]{5,4,3,2,1,0:T(8,128)(2,1)} %dynamic-slice_bitcast_fusion.10), channel_id=1, source_target_pairs={{0,1},{1,0},{2,3},{3,2},{4,5},{5,4},{6,7},{7,6},{8,9},{9,8},{10,11... | collective-permute-start | bytes 3145736 | tf_op jit(solution)/shard_map/ppermute | solution.py:56
  480.4 52.2 %collective-permute-start.53 = (bf16[2,2,2,72,1024]{4,3,2,1,0:T(8,128)(2,1)}, bf16[2,2,2,72,1024]{4,3,2,1,0:T(8,128)(2,1)}, u32[]{:S(2)}, u32[]{:S(2)}) collective-permute-start(bf16[2,2,2,72,1024]{4,3,2,1,0:T(8,128)(2,1)} %dynamic-slice_bitcast_fusion.4), channel_id=1, source_target_pairs={{0,4},{1,5},{2,6},{3,7},{4,0},{5,1},{6,2},{7,3},{8,12},{9,13},{10,... | collective-permute-start | bytes 3538952 | tf_op jit(solution)/shard_map/ppermute | solution.py:56
  482.8 52.4 %collective-permute-start.52 = (bf16[2,2,2,72,1024]{4,3,1,0,2:T(8,128)(2,1)}, bf16[2,2,2,72,1024]{4,3,1,0,2:T(8,128)(2,1)}, u32[]{:S(2)}, u32[]{:S(2)}) collective-permute-start(bf16[2,2,2,72,1024]{4,3,1,0,2:T(8,128)(2,1)} %dynamic-slice_bitcast_fusion.5), channel_id=1, source_target_pairs={{0,2},{1,3},{2,0},{3,1},{4,6},{5,7},{6,4},{7,5},{8,10},{9,11},{10,... | collective-permute-start | bytes 3538952 | tf_op jit(solution)/shard_map/ppermute | solution.py:56
  504.6 60.7 %collective-permute-start.56 = (bf16[2,2,2,2,96,1024]{5,4,3,2,1,0:T(8,128)(2,1)}, bf16[2,2,2,2,96,1024]{5,4,3,2,1,0:T(8,128)(2,1)}, u32[]{:S(2)}, u32[]{:S(2)}) collective-permute-start(bf16[2,2,2,2,96,1024]{5,4,3,2,1,0:T(8,128)(2,1)} %dynamic-slice_bitcast_fusion.3), channel_id=1, source_target_pairs={{0,1},{1,0},{2,3},{3,2},{4,5},{5,4},{6,7},{7,6},{8,9},{9,8},{10,11... | collective-permute-start | bytes 9437192 | tf_op jit(solution)/shard_map/ppermute | solution.py:56
  505.6 31.9 %collective-permute-start.55 = (bf16[2,2,2,16,1024]{4,3,2,1,0:T(8,128)(2,1)}, bf16[2,2,2,16,1024]{4,3,2,1,0:T(8,128)(2,1)}, u32[]{:S(2)}, u32[]{:S(2)}) collective-permute-start(bf16[2,2,2,16,1024]{4,3,2,1,0:T(8,128)(2,1)} %dynamic-slice_bitcast_fusion.28), channel_id=1, source_target_pairs={{0,4},{1,5},{2,6},{3,7},{4,0},{5,1},{6,2},{7,3},{8,12},{9,13},{10,... | collective-permute-start | bytes 786440 | tf_op jit(solution)/shard_map/ppermute | solution.py:56
  537.6 27.6 %collective-permute-start.49 = (bf16[2,32,4608]{2,1,0:T(8,128)(2,1)S(1)}, bf16[2,32,4608]{2,1,0:T(8,128)(2,1)S(1)}, u32[]{:S(2)}, u32[]{:S(2)}) collective-permute-start(bf16[2,32,4608]{2,1,0:T(8,128)(2,1)S(1)} %dynamic-slice_bitcast_fusion.19), channel_id=1, source_target_pairs={{0,16},{8,24},{16,0},{24,8},{1,17},{9,25},{17,1},{25,9},{2,18},{10... | collective-permute-start | bytes 1769480 | tf_op jit(solution)/shard_map/ppermute | solution.py:56
  570.3 58.7 %collective-permute-start.69 = (bf16[2,2,2,48,1024]{4,3,2,1,0:T(8,128)(2,1)}, bf16[2,2,2,48,1024]{4,3,2,1,0:T(8,128)(2,1)S(1)}, u32[]{:S(2)}, u32[]{:S(2)}) collective-permute-start(bf16[2,2,2,48,1024]{4,3,2,1,0:T(8,128)(2,1)} %dynamic-slice_bitcast_fusion.11), channel_id=1, source_target_pairs={{0,4},{1,5},{2,6},{3,7},{4,0},{5,1},{6,2},{7,3},{8,12},{9,13},{10,... | collective-permute-start | bytes 2359304 | tf_op jit(solution)/shard_map/ppermute | solution.py:56
  572.0 57.4 %collective-permute-start.68 = (bf16[2,2,2,48,1024]{4,3,1,0,2:T(8,128)(2,1)}, bf16[2,2,2,48,1024]{4,3,1,0,2:T(8,128)(2,1)S(1)}, u32[]{:S(2)}, u32[]{:S(2)}) collective-permute-start(bf16[2,2,2,48,1024]{4,3,1,0,2:T(8,128)(2,1)} %dynamic-slice_bitcast_fusion.12), channel_id=1, source_target_pairs={{0,2},{1,3},{2,0},{3,1},{4,6},{5,7},{6,4},{7,5},{8,10},{9,11},{10,... | collective-permute-start | bytes 2359304 | tf_op jit(solution)/shard_map/ppermute | solution.py:56
  573.0 17.5 %collective-permute-start.66 = (bf16[2,2,16,1024]{3,2,1,0:T(8,128)(2,1)S(1)}, bf16[2,2,16,1024]{3,2,1,0:T(8,128)(2,1)S(1)}, u32[]{:S(2)}, u32[]{:S(2)}) collective-permute-start(bf16[2,2,16,1024]{3,2,1,0:T(8,128)(2,1)S(1)} %dynamic-slice_bitcast_fusion.33), channel_id=1, source_target_pairs={{0,4},{1,5},{2,6},{3,7},{4,0},{5,1},{6,2},{7,3},{8,12},{9,13},{10,... | collective-permute-start | bytes 393224 | tf_op jit(solution)/shard_map/ppermute | solution.py:56
  574.6 17.4 %collective-permute-start.67 = (bf16[2,2,16,1024]{3,2,1,0:T(8,128)(2,1)}, bf16[2,2,16,1024]{3,2,1,0:T(8,128)(2,1)S(1)}, u32[]{:S(2)}, u32[]{:S(2)}) collective-permute-start(bf16[2,2,16,1024]{3,2,1,0:T(8,128)(2,1)} %dynamic-slice_bitcast_fusion.32), channel_id=1, source_target_pairs={{0,2},{1,3},{2,0},{3,1},{4,6},{5,7},{6,4},{7,5},{8,10},{9,11},{10,... | collective-permute-start | bytes 393224 | tf_op jit(solution)/shard_map/ppermute | solution.py:56
  575.9 27.5 %collective-permute-start.64 = (bf16[2,2,72,1024]{3,2,1,0:T(8,128)(2,1)}, bf16[2,2,72,1024]{3,2,1,0:T(8,128)(2,1)}, u32[]{:S(2)}, u32[]{:S(2)}) collective-permute-start(bf16[2,2,72,1024]{3,2,1,0:T(8,128)(2,1)} %dynamic-slice_bitcast_fusion.15), channel_id=1, source_target_pairs={{0,4},{1,5},{2,6},{3,7},{4,0},{5,1},{6,2},{7,3},{8,12},{9,13},{10,... | collective-permute-start | bytes 1769480 | tf_op jit(solution)/shard_map/ppermute | solution.py:56
  599.5 29.2 %collective-permute-start.63 = (bf16[2,144,1024]{2,1,0:T(8,128)(2,1)S(1)}, bf16[2,144,1024]{2,1,0:T(8,128)(2,1)S(1)}, u32[]{:S(2)}, u32[]{:S(2)}) collective-permute-start(bf16[2,144,1024]{2,1,0:T(8,128)(2,1)S(1)} %dynamic-slice_bitcast_fusion.16), channel_id=1, source_target_pairs={{0,16},{8,24},{16,0},{24,8},{1,17},{9,25},{17,1},{25,9},{2,18},{10... | collective-permute-start | bytes 1769480 | tf_op jit(solution)/shard_map/ppermute | solution.py:56
  629.7 24.1 %collective-permute-start.75 = (bf16[2,2,48,1024]{3,2,1,0:T(8,128)(2,1)S(1)}, bf16[2,2,48,1024]{3,2,1,0:T(8,128)(2,1)S(1)}, u32[]{:S(2)}, u32[]{:S(2)}) collective-permute-start(bf16[2,2,48,1024]{3,2,1,0:T(8,128)(2,1)S(1)} %dynamic-slice_bitcast_fusion.24), channel_id=1, source_target_pairs={{0,4},{1,5},{2,6},{3,7},{4,0},{5,1},{6,2},{7,3},{8,12},{9,13},{10,... | collective-permute-start | bytes 1179656 | tf_op jit(solution)/shard_map/ppermute | solution.py:56
  630.9 23.1 %collective-permute-start.76 = (bf16[2,2,48,1024]{3,2,1,0:T(8,128)(2,1)S(1)}, bf16[2,2,48,1024]{3,2,1,0:T(8,128)(2,1)S(1)}, u32[]{:S(2)}, u32[]{:S(2)}) collective-permute-start(bf16[2,2,48,1024]{3,2,1,0:T(8,128)(2,1)S(1)} %dynamic-slice_bitcast_fusion.23), channel_id=1, source_target_pairs={{0,2},{1,3},{2,0},{3,1},{4,6},{5,7},{6,4},{7,5},{8,10},{9,11},{10,... | collective-permute-start | bytes 1179656 | tf_op jit(solution)/shard_map/ppermute | solution.py:56
  632.4 32.4 %collective-permute-start.73 = (bf16[2,144,1024]{2,1,0:T(8,128)(2,1)S(1)}, bf16[2,144,1024]{2,1,0:T(8,128)(2,1)S(1)}, u32[]{:S(2)}, u32[]{:S(2)}) collective-permute-start(bf16[2,144,1024]{2,1,0:T(8,128)(2,1)S(1)} %dynamic-slice_bitcast_fusion.13), channel_id=1, source_target_pairs={{0,16},{8,24},{16,0},{24,8},{1,17},{9,25},{17,1},{25,9},{2,18},{10... | collective-permute-start | bytes 1769480 | tf_op jit(solution)/shard_map/ppermute | solution.py:56
  634.8 19.0 %collective-permute-start.72 = (bf16[144,1024]{1,0:T(8,128)(2,1)S(1)}, bf16[144,1024]{1,0:T(8,128)(2,1)S(1)}, u32[]{:S(2)}, u32[]{:S(2)}) collective-permute-start(bf16[144,1024]{1,0:T(8,128)(2,1)S(1)} %dynamic-slice_bitcast_fusion.26), channel_id=1, source_target_pairs={{0,8},{8,0},{16,24},{24,16},{1,9},{9,1},{17,25},{25,17},{2,10},{10... | collective-permute-start | bytes 884744 | tf_op jit(solution)/shard_map/ppermute | solution.py:56
  665.1 19.1 %collective-permute-start.83 = (bf16[2,96,1024]{2,1,0:T(8,128)(2,1)S(1)}, bf16[2,96,1024]{2,1,0:T(8,128)(2,1)S(1)}, u32[]{:S(2)}, u32[]{:S(2)}) collective-permute-start(bf16[2,96,1024]{2,1,0:T(8,128)(2,1)S(1)} %dynamic-slice_bitcast_fusion.22), channel_id=1, source_target_pairs={{0,16},{8,24},{16,0},{24,8},{1,17},{9,25},{17,1},{25,9},{2,18},{10... | collective-permute-start | bytes 1179656 | tf_op jit(solution)/shard_map/ppermute | solution.py:56
  (153 other events, 2914.6 us)
